TPU v7x, 32 devices: a whole 2x2x4 slice. The times are simulated.
32 devices in a mesh: ctx: 8 (over y, x, core), head: 4 (over z).
Axes of the slice: x: 2, y: 2, z: 4, core: 2. Of those that a mesh axis runs over, the one named last changes fastest.
Arguments:
- query_rows: bfloat16 [8192, 4096], P('ctx', 'head'), may hold values from -6 to 6
- key_rows: bfloat16 [8192, 4096], P('ctx', 'head'), may hold values from -6 to 6
- value_rows: bfloat16 [8192, 4096], P('ctx', 'head'), may hold values from -6 to 6
- frequencies: bfloat16 [32, 128, 128], P('head'), may hold values from -4.1875 to 4.1875
- norm_gain: bfloat16 [4096], P('head'), may hold values from 0.25 to 1.75
- out_weight: bfloat16 [4096, 4096], P(None, 'head'), may hold values from -0.09375 to 0.09375
Outputs:
- projected: bfloat16 [8192, 4096], P('ctx', 'head')
All inputs are finite; a program needn't handle non-finite values.
Results may differ from a plain program's by a relative error of at most 0.009.
Values may be sent and summed in bfloat16 or wider, within the bound.
No kernel may reach another device: no remote copies, remote signals or barrier semaphores. Data moves between devices by JAX's collectives and lax.ppermute only.
A program may use at most 128 MiB of HBM per device.

v0:
```python
import functools
import math

import jax
import jax.numpy as jnp
from jax import lax
from jax.experimental import pallas as pl
from jax.experimental.pallas import tpu as pltpu
from jax.sharding import PartitionSpec as P

F32 = jnp.float32
BF16 = jnp.bfloat16
SPAN = 512
TILE = 256
SIN_TERMS = (3.1406400334639137, -5.136905232797424, 2.2995469238543222)
COS_TERMS = (0.9999932955183647, -4.933938020185013, 4.0412838463445455, -1.2221270624224843)
ROUNDER = 1.5 * 2.0**23
LARGE = pltpu.CompilerParams(vmem_limit_bytes=56 << 20)
MIDDLE = pltpu.CompilerParams(vmem_limit_bytes=52 << 20)
SMALL = pltpu.CompilerParams(vmem_limit_bytes=20 << 20)
FREE = pl.CostEstimate(flops=0, bytes_accessed=0, transcendentals=0)


def dot(a, b, contract):
    return lax.dot_general(a, b, ((contract[:1], contract[1:]), ((), ())), preferred_element_type=F32)


def poly(terms, scale, u):
    value = F32(terms[-1] * scale)
    for term in terms[-2::-1]:
        value = value * u + F32(term * scale)
    return value


def cos_sin(phase, amplitude):
    turns = phase * F32(1.0 / (2.0 * math.pi))
    part = turns - ((turns + F32(ROUNDER)) - F32(ROUNDER))
    u = part * part
    scale = math.sqrt(2.0 * amplitude)
    half_sin = poly(SIN_TERMS, scale, u) * part
    half_cos = poly(COS_TERMS, scale, u)
    return F32(amplitude) - half_sin * half_sin, half_sin * half_cos


def key_kernel(has_weight, core_ref, place_ref, turn_ref, key_ref, value_ref, freq_ref, *refs):
    if has_weight:
        refs[-1][...] = refs[0][...]
        refs = refs[1:]
    feat_ref, sent_ref, kept_ref, prefix_ref = refs[:4]
    rows = key_ref.shape[0]
    group, width, count = freq_ref.shape
    span = min(SPAN, rows)
    amplitude = 1.0 / math.sqrt(count)
    tiles = [(head, start) for head in range(group) for start in range(0, rows, TILE)]
    turned = [freq_ref[head].T for head in range(group)]

    def phase_of(head, start):
        lanes = slice(head * width, (head + 1) * width)
        return dot(turned[head], key_ref[start : start + TILE, lanes], (1, 1))

    def add_state(head, start, features):
        lanes = slice(head * width, (head + 1) * width)
        state = dot(features, value_ref[start : start + TILE, lanes], (1, 0))
        sums[head] = state if start == 0 else sums[head] + state
        index = (start + TILE) // span - 1
        if (start + TILE) % span == 0 and index < prefix_ref.shape[1]:
            prefix_ref[head, index] = sums[head]

    sums = [None] * group
    phase, waiting = phase_of(*tiles[0]), None
    for index, (head, start) in enumerate(tiles):
        following = phase_of(*tiles[index + 1]) if index + 1 < len(tiles) else None
        cosine, sine = cos_sin(phase, amplitude)
        features = jnp.concatenate([cosine.astype(BF16), sine.astype(BF16)], axis=0)
        feat_ref[head, :, start : start + TILE] = features
        if waiting is not None:
            add_state(*waiting)
        phase, waiting = following, (head, start, features)
    add_state(*waiting)
    sums = [total.astype(BF16) for total in sums]
    half = pl.num_programs(0) // 2

    @pl.when(pl.program_id(0) < half)
    def _():
        for head in range(group):
            sent_ref[head] = sums[head]

    @pl.when(pl.program_id(0) >= half)
    def _():
        for head in range(group):
            kept_ref[head] = sums[head]


def key_side(core, place, turn, key_rows, value_rows, frequencies, weight=None):
    rows = key_rows.shape[0]
    heads, width, count = frequencies.shape
    prior = max(1, rows // min(SPAN, rows) - 1)
    half = heads // 2
    group = 2 if half % 2 == 0 else 1
    steps, half_steps = heads // group, half // group

    def block(g, c):
        return (g + half_steps * (1 - c[0])) % steps

    in_specs = [
        pl.BlockSpec((rows, group * width), lambda g, c, p, t: (0, block(g, c))),
        pl.BlockSpec((rows, group * width), lambda g, c, p, t: (0, block(g, c))),
        pl.BlockSpec((group, width, count), lambda g, c, p, t: (block(g, c), 0, 0)),
    ]
    out_specs = [
        pl.BlockSpec((group, 2 * count, rows), lambda g, c, p, t: (block(g, c), 0, 0)),
        pl.BlockSpec((group, 2 * count, width), lambda g, c, p, t: (jnp.minimum(g, half_steps - 1), 0, 0)),
        pl.BlockSpec((group, 2 * count, width), lambda g, c, p, t: (jnp.maximum(g - half_steps, 0), 0, 0)),
        pl.BlockSpec((group, prior, 2 * count, width), lambda g, c, p, t: (block(g, c), 0, 0, 0)),
    ]
    out_shape = [
        jax.ShapeDtypeStruct((heads, 2 * count, rows), BF16),
        jax.ShapeDtypeStruct((half, 2 * count, width), BF16),
        jax.ShapeDtypeStruct((half, 2 * count, width), BF16),
        jax.ShapeDtypeStruct((heads, prior, 2 * count, width), F32),
    ]
    operands = [key_rows, value_rows, frequencies]
    if weight is not None:
        depth, cols = weight.shape[0] // 4, weight.shape[1]
        piece = depth // 2 // steps

        def rows_of(g, c, p, t):
            return ((p[0] ^ (1 + 2 * c[0])) * 2 + t[0]) * steps + g, 0

        in_specs.append(pl.BlockSpec((piece, cols), rows_of))
        out_specs.append(pl.BlockSpec((piece, cols), lambda g, c, p, t: (g, 0)))
        out_shape.append(jax.ShapeDtypeStruct((depth // 2, cols), weight.dtype))
        operands.append(weight)
    return pl.pallas_call(
        functools.partial(key_kernel, weight is not None),
        grid_spec=pltpu.PrefetchScalarGridSpec(
            num_scalar_prefetch=3, grid=(steps,), in_specs=in_specs, out_specs=out_specs
        ),
        out_shape=out_shape,
        compiler_params=LARGE,
        cost_estimate=FREE,
        name="key_side",
    )(core, place, turn, *operands)


def query_kernel(query_ref, value_ref, freq_ref, key_feat_ref, feat_ref, local_ref):
    rows = query_ref.shape[0]
    group, width, count = freq_ref.shape
    span = min(SPAN, rows)
    amplitude = 1.0 / math.sqrt(count)
    below = lax.broadcasted_iota(jnp.int32, (TILE, TILE), 0)
    causal = below >= lax.broadcasted_iota(jnp.int32, (TILE, TILE), 1)
    tiles = [(head, start) for head in range(group) for start in range(0, rows, TILE)]

    def phase_of(head, start):
        lanes = slice(head * width, (head + 1) * width)
        return dot(query_ref[start : start + TILE, lanes], freq_ref[head], (1, 0))

    def attend(head, start, features):
        lanes = slice(head * width, (head + 1) * width)
        total = None
        for other in range(start // span * span, start + TILE, TILE):
            theirs = slice(other, other + TILE)
            scores = dot(features, key_feat_ref[head, :, theirs], (1, 0))
            if other == start:
                scores = jnp.where(causal, scores, F32(0.0))
            part = dot(scores.astype(BF16), value_ref[theirs, lanes], (1, 0))
            total = part if total is None else total + part
        local_ref[start : start + TILE, lanes] = total.astype(local_ref.dtype)

    phase, waiting = phase_of(*tiles[0]), None
    for index, (head, start) in enumerate(tiles):
        following = phase_of(*tiles[index + 1]) if index + 1 < len(tiles) else None
        cosine, sine = cos_sin(phase, amplitude)
        features = jnp.concatenate([cosine.astype(BF16), sine.astype(BF16)], axis=1)
        feat_ref[head, start : start + TILE, :] = features
        if waiting is not None:
            attend(*waiting)
        phase, waiting = following, (head, start, features)
    attend(*waiting)


def query_side(query_rows, value_rows, frequencies, key_feat):
    rows = query_rows.shape[0]
    heads, width, count = frequencies.shape
    group = 2 if heads % 2 == 0 else 1
    return pl.pallas_call(
        query_kernel,
        grid=(heads // group,),
        in_specs=[
            pl.BlockSpec((rows, group * width), lambda h: (0, h)),
            pl.BlockSpec((rows, group * width), lambda h: (0, h)),
            pl.BlockSpec((group, width, count), lambda h: (h, 0, 0)),
            pl.BlockSpec((group, 2 * count, rows), lambda h: (h, 0, 0)),
        ],
        out_specs=[
            pl.BlockSpec((group, rows, 2 * count), lambda h: (h, 0, 0)),
            pl.BlockSpec((rows, group * width), lambda h: (0, h)),
        ],
        out_shape=[
            jax.ShapeDtypeStruct((heads, rows, 2 * count), BF16),
            jax.ShapeDtypeStruct((rows, heads * width), BF16),
        ],
        compiler_params=LARGE,
        cost_estimate=FREE,
        name="query_side",
    )(query_rows, value_rows, frequencies, key_feat)


def finish_kernel(
    heads, span, cuts, core_ref, feat_ref, local_ref, theirs_ref, mine_ref, gain_ref, *refs
):
    prefix_ref, out_refs = refs[0], refs[-len(cuts) :]
    width = local_ref.shape[1] // heads
    steps = pl.num_programs(0)
    kept = pl.program_id(0) >= steps // 2
    first_head = lax.rem(pl.program_id(0) + steps // 2 * (1 - core_ref[0]), steps) * heads
    gains = gain_ref[...].astype(F32)
    row = lax.broadcasted_iota(jnp.int32, gains.shape, 0)
    for head in range(heads):
        cols = slice(head * width, (head + 1) * width)
        gain = jnp.sum(jnp.where(row == first_head + head, gains, F32(0.0)), axis=0, keepdims=True)
        before = jnp.where(kept, mine_ref[head].astype(F32), theirs_ref[head].astype(F32))
        for out_ref, (first, last) in zip(out_refs, cuts):
            starts = [first, *range(first - first % TILE + TILE, last, TILE)]
            for start, stop in zip(starts, starts[1:] + [last]):
                mine = slice(start, stop)
                carried = before
                if start // span:
                    carried = carried + prefix_ref[head, start // span - 1]
                prior = dot(feat_ref[head, mine, :], carried.astype(BF16), (1, 0))
                attended = local_ref[mine, cols].astype(F32) + prior
                square = jnp.mean(attended * attended, axis=-1, keepdims=True)
                normed = attended * lax.rsqrt(square + F32(1e-6)) * gain
                out_ref[start - first : stop - first, cols] = normed.astype(BF16)


def finish(core, feat, local_part, theirs, mine, gain, prefix, cuts):
    heads, all_rows, feats = feat.shape
    rows = cuts[-1][1]
    span = min(SPAN, all_rows)
    width = local_part.shape[1] // heads
    prior = prefix.shape[1]
    half = heads // 2
    group = 4 if half % 4 == 0 and rows < span else 2 if half % 2 == 0 else 1
    steps, half_steps = heads // group, half // group

    def block(g, c):
        return (g + half_steps * (1 - c[0])) % steps

    in_specs = [
        pl.BlockSpec((group, rows, feats), lambda g, c: (block(g, c), 0, 0)),
        pl.BlockSpec((rows, group * width), lambda g, c: (0, block(g, c))),
        pl.BlockSpec((group, feats, width), lambda g, c: (jnp.minimum(g, half_steps - 1), 0, 0)),
        pl.BlockSpec((group, feats, width), lambda g, c: (jnp.maximum(g - half_steps, 0), 0, 0)),
        pl.BlockSpec(gain.shape, lambda g, c: (0, 0)),
    ]
    operands = [feat, local_part, theirs, mine, gain]
    if rows > span:
        in_specs.append(pl.BlockSpec((group, prior, feats, width), lambda g, c: (block(g, c), 0, 0, 0)))
        operands.append(prefix)
    return pl.pallas_call(
        functools.partial(finish_kernel, group, span, cuts),
        grid_spec=pltpu.PrefetchScalarGridSpec(
            num_scalar_prefetch=1,
            grid=(steps,),
            in_specs=in_specs,
            out_specs=[
                pl.BlockSpec((last - first, group * width), lambda g, c: (0, block(g, c))) for first, last in cuts
            ],
        ),
        out_shape=[jax.ShapeDtypeStruct((last - first, heads * width), BF16) for first, last in cuts],
        compiler_params=LARGE if rows > span else MIDDLE,
        cost_estimate=FREE,
        name="finish",
    )(core, *operands)


def project_kernel(sources, place_ref, *refs):
    out_ref = refs[-1]
    total = None
    for x_ref, w_ref in zip(refs[:sources], refs[sources : 2 * sources]):
        part = dot(x_ref[...], w_ref[...], (1, 0))
        total = part if total is None else total + part
    out_ref[...] = total.astype(out_ref.dtype)


def project(blocks, weight, place, hops, dtype=BF16):
    size, depth = blocks[0].shape
    cols = weight.shape[1]
    step = min(512, cols)

    def rows_of(source):
        return lambda n, p: (p[0] ^ hops[source], n)

    sources = len(blocks)
    return pl.pallas_call(
        functools.partial(project_kernel, sources),
        grid_spec=pltpu.PrefetchScalarGridSpec(
            num_scalar_prefetch=1,
            grid=(cols // step,),
            in_specs=[pl.BlockSpec((size, depth), lambda n, p: (0, 0)) for _ in blocks]
            + [pl.BlockSpec((depth, step), rows_of(source)) for source in range(sources)],
            out_specs=pl.BlockSpec((size, step), lambda n, p: (0, n)),
        ),
        out_shape=jax.ShapeDtypeStruct((size, cols), dtype),
        compiler_params=SMALL,
        cost_estimate=FREE,
        name="project",
    )(place, *blocks, *[weight] * sources)


def partial_kernel(core_ref, turn_ref, x_ref, y_ref, *refs):
    weights, out_ref = refs[:-1], refs[-1]
    count = len(weights) // 2
    swapped, turned = core_ref[0] != 0, turn_ref[0] != 0
    x, y = x_ref[...], y_ref[...]
    half = x.shape[1] // 2
    total = None
    for rows, pieces in ((jnp.where(swapped, y, x), weights[:count]), (jnp.where(swapped, x, y), weights[count:])):
        left, right = rows[:, :half], rows[:, half:]
        sides = [jnp.where(turned, right, left), jnp.where(turned, left, right)]
        rows = jnp.concatenate(sides, axis=1)
        first = 0
        for piece in pieces:
            last = first + piece.shape[0]
            part = dot(rows[:, first:last], piece[...], (1, 0))
            total = part if total is None else total + part
            first = last
    out_ref[...] = total.astype(out_ref.dtype)


def partial_product(core, turn, blocks, weights):
    size, depth = blocks[0].shape
    cols = weights[0].shape[1]
    step = min(512, cols)
    return pl.pallas_call(
        partial_kernel,
        grid_spec=pltpu.PrefetchScalarGridSpec(
            num_scalar_prefetch=2,
            grid=(cols // step,),
            in_specs=[pl.BlockSpec((size, depth), lambda n, c, t: (0, 0)) for _ in blocks]
            + [pl.BlockSpec((weight.shape[0], step), lambda n, c, t: (0, n)) for weight in weights],
            out_specs=pl.BlockSpec((size, step), lambda n, c, t: (0, n)),
        ),
        out_shape=jax.ShapeDtypeStruct((size, cols), BF16),
        compiler_params=SMALL,
        cost_estimate=FREE,
        name="partial_product",
    )(core, turn, *blocks, *weights)


def join_kernel(a_ref, b_ref, *refs):
    out_ref = refs[-1]
    out_ref[...] = (a_ref[...] + b_ref[...].astype(F32)).astype(out_ref.dtype)


def join(a, b, first, rows, into=None):
    size, cols = a.shape
    step = math.gcd(first, size, 256)
    index = first // step
    spec = pl.BlockSpec((step, cols), lambda r: (r, 0))
    return pl.pallas_call(
        join_kernel,
        grid=(size // step,),
        in_specs=[spec, spec] + [pl.BlockSpec(memory_space=pl.ANY)] * (into is not None),
        out_specs=pl.BlockSpec((step, cols), lambda r: (index + r, 0)),
        out_shape=jax.ShapeDtypeStruct((rows, cols), BF16),
        input_output_aliases={} if into is None else {2: 0},
        compiler_params=SMALL,
        cost_estimate=FREE,
        name="join",
    )(a, b, *([] if into is None else [into]))


def after(value, *others):
    return lax.optimization_barrier((value, *others))[0]


def swap(value, axis, distance):
    return lax.ppermute(value, axis, [(i, i ^ distance) for i in range(lax.axis_size(axis))])


def earlier_states(sent, kept, meanwhile):
    count, mine = lax.axis_size("ctx"), lax.axis_index("ctx")
    core = mine % 2
    partner = swap(sent, "ctx", 1)
    total = (kept.astype(F32) + partner.astype(F32)).astype(BF16)
    earlier = jnp.zeros(kept.shape, F32)
    beside = meanwhile(total)
    distance = 2
    while distance < count:
        radix = min(4, count // distance)
        last = distance * radix >= count
        added = total.astype(F32)
        for step in range(1, radix):
            hop = step * distance
            pairs = [(i, i ^ hop) for i in range(count) if not last or i < i ^ hop]
            theirs = lax.ppermute(total, "ctx", pairs)
            if last:
                theirs = after(theirs, *beside)
            theirs = theirs.astype(F32)
            lower = (mine ^ hop) < mine
            earlier = earlier + jnp.where(lower, theirs, F32(0.0))
            added = added + theirs
        total = added.astype(BF16)
        distance *= radix
    own = earlier + jnp.where(core == 1, partner.astype(F32), F32(0.0))
    given = earlier + jnp.where(core == 0, kept.astype(F32), F32(0.0))
    return swap(given.astype(BF16), "ctx", 1), own.astype(BF16), beside


def normed_output(core, place, turn, query_rows, key_rows, value_rows, frequencies, norm_gain, weight=None):
    key_feat, sent, kept, prefix, *share = key_side(core, place, turn, key_rows, value_rows, frequencies, weight)

    gain = norm_gain.reshape(frequencies.shape[0], -1)

    def meanwhile(total):
        return query_side(query_rows, value_rows, after(frequencies, total), key_feat)

    theirs, own, (query_feat, local_part) = earlier_states(sent, kept, meanwhile)

    def blocks_of(cuts, *others):
        return finish(core, after(query_feat, *others), local_part, theirs, own, gain, prefix, cuts)

    return blocks_of, share


def positions():
    spot, place = lax.axis_index("ctx"), lax.axis_index("head")
    return [value.astype(jnp.int32).reshape(1) for value in (spot % 2, place, (spot // 2 + spot // 4) % 2)]


def line_of_four(query_rows, key_rows, value_rows, frequencies, norm_gain, out_weight):
    rows = query_rows.shape[0]
    core, place, turn = positions()
    sizes = [rows * part // 16 for part in (2,) * 8]
    edges = [sum(sizes[:i]) for i in range(len(sizes) + 1)]
    cuts = tuple(zip(edges[:-1], edges[1:]))
    parts = (query_rows, key_rows, value_rows, frequencies, norm_gain)
    blocks_of, (share,) = normed_output(core, place, turn, *parts, out_weight)
    blocks = blocks_of(cuts[:1])
    share = after(swap(share, "head", 1), *blocks)
    half = share.shape[0] // 2
    halves = [share[:half], share[half:]]
    blocks = [*blocks, *blocks_of(cuts[1:], *halves)]
    pairs, given, partials, products = [], [], [], []
    out, joined = None, 0
    for index, block in enumerate(blocks):
        if index > 2:
            block = after(block, given[index - 2], partials[max(0, index - 4)], products[max(0, index - 4)])
        if index == len(blocks) - 1:
            while joined < index - 4:
                out = join(after(products[joined], given[index - 2]), partials[joined], cuts[joined][0], rows, out)
                joined += 1
            block, out = lax.optimization_barrier((block, out))
        pairs.append([block, swap(block, "head", 2)])
        if index == 1:
            others = [swap(part, "ctx", hop) for part, hop in zip(halves, (2, 4))]
            shares = [after(share, blocks[-1], pairs[0][1])] + [after(other, pairs[0][1]) for other in others]
            weights = shares + [swap(part, "ctx", 1) for part in shares]
            x, y = pairs[0]
            given.append(partial_product(core, turn, [x, y], weights))
            x, y = pairs[1]
            given.append(partial_product(core, turn, [x, after(y, given[0])], weights))
        elif index > 1:
            x, y = pairs[-1]
            y = after(y, partials[index - 2], given[-1], *(products[:-1] if index == len(blocks) - 1 else []))
            given.append(partial_product(core, turn, [x, y], weights))
        partials += [swap(part, "head", 1) for part in given[len(partials) :]]
        products.append(project(pairs[-1], out_weight, place, (0, 2), F32))
    for product, partial, (first, _) in list(zip(products, partials, cuts))[joined:]:
        out = join(product, partial, first, rows, out)
    return out


def any_line(query_rows, key_rows, value_rows, frequencies, norm_gain, out_weight):
    core, place, turn = positions()
    parts = (query_rows, key_rows, value_rows, frequencies, norm_gain)
    blocks_of, _ = normed_output(core, place, turn, *parts)
    (normed,) = blocks_of(((0, query_rows.shape[0]),))
    gathered = lax.all_gather(normed, "head", axis=1, tiled=True)
    return jnp.dot(gathered, out_weight, preferred_element_type=F32).astype(BF16)


def solution(mesh):
    return jax.shard_map(
        line_of_four if mesh.shape["head"] == 4 and mesh.shape["ctx"] % 8 == 0 else any_line,
        mesh=mesh,
        in_specs=(
            P("ctx", "head"),
            P("ctx", "head"),
            P("ctx", "head"),
            P("head", None, None),
            P("head"),
            P(None, "head"),
        ),
        out_specs=P("ctx", "head"),
        check_vma=False,
    )
```

profile of v0, /device:TPU:0, one launch (start us, length us, event | category | flops | bytes accessed | tf_op | source)
XLA Modules:
  0.0 148.0 jit_solution(9940320607790685205)
XLA Ops:
  0.0 8.2 %key_side.1 = (bf16[8,256,1024]{2,1,0:T(8,128)(2,1)}, bf16[4,256,128]{2,1,0:T(8,128)(2,1)}, bf16[4,256,128]{2,1,0:T(8,128)(2,1)}, f32[8,1,256,128]{3,2,1,0:T(8,128)}, bf16[512,1024]{1,0:T(8,128)(2,1)}) custom-call(s32[1]{0:T(128)} %bitcast.1.core_ref, s32[1]{0:T(128)} %bitcast.place_ref, s32[1]{0:T(128)} %bitcast.2.turn_ref, bf16[1024,1024]{1,0:T(8,128)(2,1)} %key_ref.1, ...), custom_call_target="tpu_custom_call" | custom-call | tf_op jit(solution)/shard_map/key_side/pallas_call | solution.py:134
  8.7 2.6 %collective-permute-start.1 = (bf16[512,1024]{1,0:T(8,128)(2,1)}, bf16[512,1024]{1,0:T(8,128)(2,1)S(1)}, u32[]{:S(2)}, u32[]{:S(2)}) collective-permute-start(bf16[512,1024]{1,0:T(8,128)(2,1)} %get-tuple-element.50), channel_id=1, source_target_pairs={{0,1},{1,0},{2,3},{3,2},{4,5},{5,4},{6,7},{7,6},{8,9},{9,8},{10,11... | collective-permute-start | bytes 3145736 | tf_op jit(solution)/shard_map/ppermute | solution.py:381
  12.3 3.5 %collective-permute-start.2 = (bf16[4,256,128]{2,1,0:T(8,128)(2,1)S(1)}, bf16[4,256,128]{2,1,0:T(8,128)(2,1)S(1)}, u32[]{:S(2)}, u32[]{:S(2)}) collective-permute-start(bf16[4,256,128]{2,1,0:T(8,128)(2,1)S(1)} %fusion.2), channel_id=1, source_target_pairs={{0,8},{4,12},{16,24},{20,28},{1,9},{5,13},{17,25},{21,29},{2,10},{... | collective-permute-start | bytes 786440 | tf_op jit(solution)/shard_map/ppermute | solution.py:399
  15.8 3.4 %collective-permute-start.3 = (bf16[4,256,128]{2,1,0:T(8,128)(2,1)S(1)}, bf16[4,256,128]{2,1,0:T(8,128)(2,1)S(1)}, u32[]{:S(2)}, u32[]{:S(2)}) collective-permute-start(bf16[4,256,128]{2,1,0:T(8,128)(2,1)S(1)} %fusion.2), channel_id=1, source_target_pairs={{0,16},{4,20},{8,24},{12,28},{1,17},{5,21},{9,25},{13,29},{2,18},{... | collective-permute-start | bytes 786440 | tf_op jit(solution)/shard_map/ppermute | solution.py:399
  19.3 1.3 collective-permute-start.4
  20.6 9.8 %query_side.1 = (bf16[8,1024,256]{2,1,0:T(8,128)(2,1)}, bf16[1024,1024]{1,0:T(8,128)(2,1)}) custom-call(bf16[1024,1024]{1,0:T(8,128)(2,1)} %query_ref.1, bf16[1024,1024]{1,0:T(8,128)(2,1)} %value_ref.3, bf16[8,128,128]{2,1,0:T(8,128)(2,1)} %freq_ref.2, bf16[8,256,1024]{2,1,0:T(8,128)(2,1)} %get-tuple-element.48.key_feat_ref), custom_call_target="tpu_custom_call" | custom-call | tf_op jit(solution)/shard_map/query_side/pallas_call | solution.py:187
  30.9 1.5 %collective-permute-done.5.theirs_ref = bf16[4,256,128]{2,1,0:T(8,128)(2,1)S(1)} collective-permute-done((bf16[4,256,128]{2,1,0:T(8,128)(2,1)S(1)}, bf16[4,256,128]{2,1,0:T(8,128)(2,1)S(1)}, u32[]{:S(2)}, u32[]{:S(2)}) %collective-permute-start.5) | collective-permute-done | bytes 262176 | tf_op jit(solution)/shard_map/ppermute | solution.py:381
  32.4 1.8 %finish.2.x_ref.refs_0_ = bf16[128,1024]{1,0:T(8,128)(2,1)S(1)} custom-call(s32[1]{0:T(128)} %bitcast.1.core_ref, bf16[8,1024,256]{2,1,0:T(8,128)(2,1)} %get-tuple-element.56.feat_ref, bf16[1024,1024]{1,0:T(8,128)(2,1)} %get-tuple-element.51.local_ref, bf16[4,256,128]{2,1,0:T(8,128)(2,1)S(1)} %collective-permute-done.5.theirs_ref, ...), custom_call_target="tpu_custom_call" | custom-call | tf_op jit(solution)/shard_map/finish/pallas_call | solution.py:262
  34.2 2.7 %collective-permute-start.7 = (bf16[128,1024]{1,0:T(8,128)(2,1)S(1)}, bf16[128,1024]{1,0:T(8,128)(2,1)S(1)}, u32[]{:S(2)}, u32[]{:S(2)}) collective-permute-start(bf16[128,1024]{1,0:T(8,128)(2,1)S(1)} %finish.2.x_ref.refs_0_), channel_id=1, source_target_pairs={{0,2},{1,3},{2,0},{3,1},{4,6},{5,7},{6,4},{7,5},{8,10},{9,11},{10,... | collective-permute-start | bytes 786440 | tf_op jit(solution)/shard_map/ppermute | solution.py:381
  37.0 2.5 %collective-permute-start.9 = (bf16[256,1024]{1,0:T(8,128)(2,1)S(1)}, bf16[256,1024]{1,0:T(8,128)(2,1)S(1)}, u32[]{:S(2)}, u32[]{:S(2)}) collective-permute-start(bf16[256,1024]{1,0:T(8,128)(2,1)S(1)} %get-tuple-element.85), channel_id=1, source_target_pairs={{0,16},{4,20},{8,24},{12,28},{16,0},{20,4},{24,8},{28,12},{1,17},{... | collective-permute-start | bytes 1572872 | tf_op jit(solution)/shard_map/ppermute | solution.py:381
  39.5 5.8 %finish.3 = (bf16[128,1024]{1,0:T(8,128)(2,1)}, bf16[128,1024]{1,0:T(8,128)(2,1)}, bf16[128,1024]{1,0:T(8,128)(2,1)}, bf16[128,1024]{1,0:T(8,128)(2,1)}, bf16[12...) custom-call(s32[1]{0:T(128)} %bitcast.1.core_ref, ...), custom_call_target="tpu_custom_call" | custom-call | tf_op jit(solution)/shard_map/finish/pallas_call | solution.py:262
  45.3 3.8 %collective-permute-done.7.y_ref.refs_1_ = bf16[128,1024]{1,0:T(8,128)(2,1)S(1)} collective-permute-done((bf16[128,1024]{1,0:T(8,128)(2,1)S(1)}, bf16[128,1024]{1,0:T(8,128)(2,1)S(1)}, u32[]{:S(2)}, u32[]{:S(2)}) %collective-permute-start.7) | collective-permute-done | bytes 262176 | tf_op jit(solution)/shard_map/ppermute | solution.py:381
  49.2 2.3 %collective-permute-done.9.refs_2_ = bf16[256,1024]{1,0:T(8,128)(2,1)S(1)} collective-permute-done((bf16[256,1024]{1,0:T(8,128)(2,1)S(1)}, bf16[256,1024]{1,0:T(8,128)(2,1)S(1)}, u32[]{:S(2)}, u32[]{:S(2)}) %collective-permute-start.9) | collective-permute-done | bytes 524320 | tf_op jit(solution)/shard_map/ppermute | solution.py:381
  51.4 1.5 collective-permute-done.8.refs_1_
  53.4 1.5 collective-permute-done.11.refs_4_
  54.8 1.3 partial_product.8
  56.1 1.6 %collective-permute-start.13 = (bf16[128,1024]{1,0:T(8,128)(2,1)S(1)}, bf16[128,1024]{1,0:T(8,128)(2,1)S(1)}, u32[]{:S(2)}, u32[]{:S(2)}) collective-permute-start(bf16[128,1024]{1,0:T(8,128)(2,1)S(1)} %partial_product.8), channel_id=1, source_target_pairs={{0,1},{1,0},{2,3},{3,2},{4,5},{5,4},{6,7},{7,6},{8,9},{9,8},{10,11... | collective-permute-start | bytes 786440 | tf_op jit(solution)/shard_map/ppermute | solution.py:381
  57.7 1.1 collective-permute-start.16
  58.8 3.4 %copy-done = bf16[4096,1024]{1,0:T(8,128)(2,1)S(1)} copy-done((bf16[4096,1024]{1,0:T(8,128)(2,1)S(1)}, bf16[4096,1024]{1,0:T(8,128)(2,1)}, u32[]{:S(2)}) %copy-start) | copy-done | bytes 8388632
  62.2 1.3 project.8.a_ref
  63.5 5.4 %collective-permute-done.6.y_ref.refs_1_ = bf16[128,1024]{1,0:T(8,128)(2,1)S(1)} collective-permute-done((bf16[128,1024]{1,0:T(8,128)(2,1)}, bf16[128,1024]{1,0:T(8,128)(2,1)S(1)}, u32[]{:S(2)}, u32[]{:S(2)}) %collective-permute-start.6) | collective-permute-done | bytes 262176 | tf_op jit(solution)/shard_map/ppermute | solution.py:381
  68.8 1.3 partial_product.9
  70.3 1.8 %collective-permute-start.14 = (bf16[128,1024]{1,0:T(8,128)(2,1)S(1)}, bf16[128,1024]{1,0:T(8,128)(2,1)S(1)}, u32[]{:S(2)}, u32[]{:S(2)}) collective-permute-start(bf16[128,1024]{1,0:T(8,128)(2,1)S(1)} %copy-done.7), channel_id=1, source_target_pairs={{0,2},{1,3},{2,0},{3,1},{4,6},{5,7},{6,4},{7,5},{8,10},{9,11},{10,... | collective-permute-start | bytes 786440 | tf_op jit(solution)/shard_map/ppermute | solution.py:381
  72.1 8.0 %collective-permute-done.16.y_ref.refs_1_ = bf16[128,1024]{1,0:T(8,128)(2,1)S(1)} collective-permute-done((bf16[128,1024]{1,0:T(8,128)(2,1)S(1)}, bf16[128,1024]{1,0:T(8,128)(2,1)S(1)}, u32[]{:S(2)}, u32[]{:S(2)}) %collective-permute-start.16) | collective-permute-done | bytes 262176 | tf_op jit(solution)/shard_map/ppermute | solution.py:381
  80.1 1.3 partial_product.10
  81.5 1.8 %collective-permute-start.20 = (bf16[128,1024]{1,0:T(8,128)(2,1)S(1)}, bf16[128,1024]{1,0:T(8,128)(2,1)S(1)}, u32[]{:S(2)}, u32[]{:S(2)}) collective-permute-start(bf16[128,1024]{1,0:T(8,128)(2,1)S(1)} %partial_product.10), channel_id=1, source_target_pairs={{0,1},{1,0},{2,3},{3,2},{4,5},{5,4},{6,7},{7,6},{8,9},{9,8},{10,11... | collective-permute-start | bytes 786440 | tf_op jit(solution)/shard_map/ppermute | solution.py:381
  83.3 1.3 project.9.a_ref
  84.6 12.3 %collective-permute-done.14.y_ref.refs_1_ = bf16[128,1024]{1,0:T(8,128)(2,1)S(1)} collective-permute-done((bf16[128,1024]{1,0:T(8,128)(2,1)S(1)}, bf16[128,1024]{1,0:T(8,128)(2,1)S(1)}, u32[]{:S(2)}, u32[]{:S(2)}) %collective-permute-start.14) | collective-permute-done | bytes 262176 | tf_op jit(solution)/shard_map/ppermute | solution.py:381
  96.9 1.3 partial_product.11
  98.3 1.4 collective-permute-start.18
  99.7 1.3 project.11.a_ref
  101.0 7.2 %collective-permute-done.19.y_ref.refs_1_ = bf16[128,1024]{1,0:T(8,128)(2,1)S(1)} collective-permute-done((bf16[128,1024]{1,0:T(8,128)(2,1)S(1)}, bf16[128,1024]{1,0:T(8,128)(2,1)S(1)}, u32[]{:S(2)}, u32[]{:S(2)}) %collective-permute-start.19) | collective-permute-done | bytes 262176 | tf_op jit(solution)/shard_map/ppermute | solution.py:381
  108.3 1.3 partial_product.12
  110.7 1.3 project.10.a_ref
  112.0 1.9 %collective-permute-done.17.y_ref.refs_1_ = bf16[128,1024]{1,0:T(8,128)(2,1)S(1)} collective-permute-done((bf16[128,1024]{1,0:T(8,128)(2,1)S(1)}, bf16[128,1024]{1,0:T(8,128)(2,1)S(1)}, u32[]{:S(2)}, u32[]{:S(2)}) %collective-permute-start.17) | collective-permute-done | bytes 262176 | tf_op jit(solution)/shard_map/ppermute | solution.py:381
  113.9 2.6 %collective-permute-done.18.b_ref = bf16[128,1024]{1,0:T(8,128)(2,1)S(1)} collective-permute-done((bf16[128,1024]{1,0:T(8,128)(2,1)S(1)}, bf16[128,1024]{1,0:T(8,128)(2,1)S(1)}, u32[]{:S(2)}, u32[]{:S(2)}) %collective-permute-start.18) | collective-permute-done | bytes 262176 | tf_op jit(solution)/shard_map/ppermute | solution.py:381
  116.5 1.3 partial_product.13
  120.3 2.1 %collective-permute-start.21 = (bf16[128,1024]{1,0:T(8,128)(2,1)S(1)}, bf16[128,1024]{1,0:T(8,128)(2,1)S(1)}, u32[]{:S(2)}, u32[]{:S(2)}) collective-permute-start(bf16[128,1024]{1,0:T(8,128)(2,1)S(1)} %copy-done.3), channel_id=1, source_target_pairs={{0,2},{1,3},{2,0},{3,1},{4,6},{5,7},{6,4},{7,5},{8,10},{9,11},{10,... | collective-permute-start | bytes 786440 | tf_op jit(solution)/shard_map/ppermute | solution.py:381
  122.4 1.3 project.13.a_ref
  123.7 4.0 %collective-permute-done.24.b_ref = bf16[128,1024]{1,0:T(8,128)(2,1)S(1)} collective-permute-done((bf16[128,1024]{1,0:T(8,128)(2,1)S(1)}, bf16[128,1024]{1,0:T(8,128)(2,1)S(1)}, u32[]{:S(2)}, u32[]{:S(2)}) %collective-permute-start.24) | collective-permute-done | bytes 262176 | tf_op jit(solution)/shard_map/ppermute | solution.py:381
  127.6 1.3 partial_product.14
  129.0 1.3 project.14.a_ref
  130.3 4.5 %collective-permute-done.22.b_ref = bf16[128,1024]{1,0:T(8,128)(2,1)S(1)} collective-permute-done((bf16[128,1024]{1,0:T(8,128)(2,1)S(1)}, bf16[128,1024]{1,0:T(8,128)(2,1)S(1)}, u32[]{:S(2)}, u32[]{:S(2)}) %collective-permute-start.22) | collective-permute-done | bytes 262176 | tf_op jit(solution)/shard_map/ppermute | solution.py:381
  134.8 1.3 collective-permute-done.21.refs_1_.y_ref
  136.1 1.3 partial_product.15
  137.4 1.3 project.15.a_ref
  140.2 1.3 project.12.a_ref
  143.0 4.3 %collective-permute-done.25.b_ref = bf16[128,1024]{1,0:T(8,128)(2,1)S(1)} collective-permute-done((bf16[128,1024]{1,0:T(8,128)(2,1)S(1)}, bf16[128,1024]{1,0:T(8,128)(2,1)S(1)}, u32[]{:S(2)}, u32[]{:S(2)}) %collective-permute-start.25) | collective-permute-done | bytes 262176 | tf_op jit(solution)/shard_map/ppermute | solution.py:381
  (63 shorter events, 10.3 us)
Async XLA Ops:
  8.2 3.1 %collective-permute-start = (bf16[4,256,128]{2,1,0:T(8,128)(2,1)}, bf16[4,256,128]{2,1,0:T(8,128)(2,1)S(1)}, u32[]{:S(2)}, u32[]{:S(2)}) collective-permute-start(bf16[4,256,128]{2,1,0:T(8,128)(2,1)} %get-tuple-element.46), channel_id=1, source_target_pairs={{0,4},{4,0},{8,12},{12,8},{16,20},{20,16},{24,28},{28,24},{1,5},{5... | collective-permute-start | bytes 786440 | tf_op jit(solution)/shard_map/ppermute | solution.py:381
  8.7 28.2 %collective-permute-start.1 = (bf16[512,1024]{1,0:T(8,128)(2,1)}, bf16[512,1024]{1,0:T(8,128)(2,1)S(1)}, u32[]{:S(2)}, u32[]{:S(2)}) collective-permute-start(bf16[512,1024]{1,0:T(8,128)(2,1)} %get-tuple-element.50), channel_id=1, source_target_pairs={{0,1},{1,0},{2,3},{3,2},{4,5},{5,4},{6,7},{7,6},{8,9},{9,8},{10,11... | collective-permute-start | bytes 3145736 | tf_op jit(solution)/shard_map/ppermute | solution.py:381
  12.3 18.1 %collective-permute-start.2 = (bf16[4,256,128]{2,1,0:T(8,128)(2,1)S(1)}, bf16[4,256,128]{2,1,0:T(8,128)(2,1)S(1)}, u32[]{:S(2)}, u32[]{:S(2)}) collective-permute-start(bf16[4,256,128]{2,1,0:T(8,128)(2,1)S(1)} %fusion.2), channel_id=1, source_target_pairs={{0,8},{4,12},{16,24},{20,28},{1,9},{5,13},{17,25},{21,29},{2,10},{... | collective-permute-start | bytes 786440 | tf_op jit(solution)/shard_map/ppermute | solution.py:399
  15.8 14.6 %collective-permute-start.3 = (bf16[4,256,128]{2,1,0:T(8,128)(2,1)S(1)}, bf16[4,256,128]{2,1,0:T(8,128)(2,1)S(1)}, u32[]{:S(2)}, u32[]{:S(2)}) collective-permute-start(bf16[4,256,128]{2,1,0:T(8,128)(2,1)S(1)} %fusion.2), channel_id=1, source_target_pairs={{0,16},{4,20},{8,24},{12,28},{1,17},{5,21},{9,25},{13,29},{2,18},{... | collective-permute-start | bytes 786440 | tf_op jit(solution)/shard_map/ppermute | solution.py:399
  19.3 11.2 %collective-permute-start.4 = (bf16[4,256,128]{2,1,0:T(8,128)(2,1)S(1)}, bf16[4,256,128]{2,1,0:T(8,128)(2,1)S(1)}, u32[]{:S(2)}, u32[]{:S(2)}) collective-permute-start(bf16[4,256,128]{2,1,0:T(8,128)(2,1)S(1)} %fusion.2), channel_id=1, source_target_pairs={{0,24},{4,28},{8,16},{12,20},{1,25},{5,29},{9,17},{13,21},{2,26},{... | collective-permute-start | bytes 786440 | tf_op jit(solution)/shard_map/ppermute | solution.py:399
  20.6 9.8 %copy-start.12 = (bf16[4,256,128]{2,1,0:T(8,128)(2,1)S(1)}, bf16[4,256,128]{2,1,0:T(8,128)(2,1)}, u32[]{:S(2)}) copy-start(bf16[4,256,128]{2,1,0:T(8,128)(2,1)} %get-tuple-element.45) | copy-start | bytes 786436
  20.6 11.7 %copy-start.11 = (bf16[1024]{0:T(1024)(128)(2,1)S(1)}, bf16[1024]{0:T(1024)(128)(2,1)}, u32[]{:S(2)}) copy-start(bf16[1024]{0:T(1024)(128)(2,1)} %param.10) | copy-start | bytes 6148
  30.8 3.5 %copy-start.2 = (bf16[4,256,128]{2,1,0:T(8,128)(2,1)}, bf16[4,256,128]{2,1,0:T(8,128)(2,1)S(1)}, u32[]{:S(2)}) copy-start(bf16[4,256,128]{2,1,0:T(8,128)(2,1)S(1)} %get-tuple-element.87.mine_ref) | copy-start | bytes 786436
  30.8 1.6 %collective-permute-start.5 = (bf16[4,256,128]{2,1,0:T(8,128)(2,1)S(1)}, bf16[4,256,128]{2,1,0:T(8,128)(2,1)S(1)}, u32[]{:S(2)}, u32[]{:S(2)}) collective-permute-start(bf16[4,256,128]{2,1,0:T(8,128)(2,1)S(1)} %get-tuple-element.88), channel_id=1, source_target_pairs={{0,4},{4,0},{8,12},{12,8},{16,20},{20,16},{24,28},{28,24},{1,5},{5... | collective-permute-start | bytes 786440 | tf_op jit(solution)/shard_map/ppermute | solution.py:381
  32.4 1.8 %copy-start.10 = (bf16[4,256,128]{2,1,0:T(8,128)(2,1)}, bf16[4,256,128]{2,1,0:T(8,128)(2,1)S(1)}, u32[]{:S(2)}) copy-start(bf16[4,256,128]{2,1,0:T(8,128)(2,1)S(1)} %collective-permute-done.5.theirs_ref) | copy-start | bytes 786436
  34.2 14.9 %collective-permute-start.7 = (bf16[128,1024]{1,0:T(8,128)(2,1)S(1)}, bf16[128,1024]{1,0:T(8,128)(2,1)S(1)}, u32[]{:S(2)}, u32[]{:S(2)}) collective-permute-start(bf16[128,1024]{1,0:T(8,128)(2,1)S(1)} %finish.2.x_ref.refs_0_), channel_id=1, source_target_pairs={{0,2},{1,3},{2,0},{3,1},{4,6},{5,7},{6,4},{7,5},{8,10},{9,11},{10,... | collective-permute-start | bytes 786440 | tf_op jit(solution)/shard_map/ppermute | solution.py:381
  37.0 14.5 %collective-permute-start.9 = (bf16[256,1024]{1,0:T(8,128)(2,1)S(1)}, bf16[256,1024]{1,0:T(8,128)(2,1)S(1)}, u32[]{:S(2)}, u32[]{:S(2)}) collective-permute-start(bf16[256,1024]{1,0:T(8,128)(2,1)S(1)} %get-tuple-element.85), channel_id=1, source_target_pairs={{0,16},{4,20},{8,24},{12,28},{16,0},{20,4},{24,8},{28,12},{1,17},{... | collective-permute-start | bytes 1572872 | tf_op jit(solution)/shard_map/ppermute | solution.py:381
  39.5 13.4 %collective-permute-start.8 = (bf16[256,1024]{1,0:T(8,128)(2,1)S(1)}, bf16[256,1024]{1,0:T(8,128)(2,1)S(1)}, u32[]{:S(2)}, u32[]{:S(2)}) collective-permute-start(bf16[256,1024]{1,0:T(8,128)(2,1)S(1)} %get-tuple-element.86), channel_id=1, source_target_pairs={{0,8},{4,12},{8,0},{12,4},{16,24},{20,28},{24,16},{28,20},{1,9},{5... | collective-permute-start | bytes 1572872 | tf_op jit(solution)/shard_map/ppermute | solution.py:381
  49.2 5.6 %collective-permute-start.10 = (bf16[512,1024]{1,0:T(8,128)(2,1)S(1)}, bf16[512,1024]{1,0:T(8,128)(2,1)S(1)}, u32[]{:S(2)}, u32[]{:S(2)}) collective-permute-start(bf16[512,1024]{1,0:T(8,128)(2,1)S(1)} %collective-permute-done.1.refs_0_), channel_id=1, source_target_pairs={{0,4},{4,0},{8,12},{12,8},{16,20},{20,16},{24,28},{28,24},{1,5},{5... | collective-permute-start | bytes 3145736 | tf_op jit(solution)/shard_map/ppermute | solution.py:381
  51.4 1.9 %collective-permute-start.12 = (bf16[256,1024]{1,0:T(8,128)(2,1)S(1)}, bf16[256,1024]{1,0:T(8,128)(2,1)S(1)}, u32[]{:S(2)}, u32[]{:S(2)}) collective-permute-start(bf16[256,1024]{1,0:T(8,128)(2,1)S(1)} %collective-permute-done.9.refs_2_), channel_id=1, source_target_pairs={{0,4},{4,0},{8,12},{12,8},{16,20},{20,16},{24,28},{28,24},{1,5},{5... | collective-permute-start | bytes 1572872 | tf_op jit(solution)/shard_map/ppermute | solution.py:381
  52.9 1.9 %collective-permute-start.11 = (bf16[256,1024]{1,0:T(8,128)(2,1)S(1)}, bf16[256,1024]{1,0:T(8,128)(2,1)S(1)}, u32[]{:S(2)}, u32[]{:S(2)}) collective-permute-start(bf16[256,1024]{1,0:T(8,128)(2,1)S(1)} %collective-permute-done.8.refs_1_), channel_id=1, source_target_pairs={{0,4},{4,0},{8,12},{12,8},{16,20},{20,16},{24,28},{28,24},{1,5},{5... | collective-permute-start | bytes 1572872 | tf_op jit(solution)/shard_map/ppermute | solution.py:381
  52.9 4.8 %copy-start.8 = (bf16[128,1024]{1,0:T(8,128)(2,1)S(1)}, bf16[128,1024]{1,0:T(8,128)(2,1)}, u32[]{:S(2)}) copy-start(bf16[128,1024]{1,0:T(8,128)(2,1)} %get-tuple-element.67.x_ref.refs_0_) | copy-start | bytes 786436
  52.9 15.9 %collective-permute-start.6 = (bf16[128,1024]{1,0:T(8,128)(2,1)}, bf16[128,1024]{1,0:T(8,128)(2,1)S(1)}, u32[]{:S(2)}, u32[]{:S(2)}) collective-permute-start(bf16[128,1024]{1,0:T(8,128)(2,1)} %get-tuple-element.61.x_ref.refs_0_), channel_id=1, source_target_pairs={{0,2},{1,3},{2,0},{3,1},{4,6},{5,7},{6,4},{7,5},{8,10},{9,11},{10,... | collective-permute-start | bytes 786440 | tf_op jit(solution)/shard_map/ppermute | solution.py:381
  56.1 14.1 %collective-permute-start.13 = (bf16[128,1024]{1,0:T(8,128)(2,1)S(1)}, bf16[128,1024]{1,0:T(8,128)(2,1)S(1)}, u32[]{:S(2)}, u32[]{:S(2)}) collective-permute-start(bf16[128,1024]{1,0:T(8,128)(2,1)S(1)} %partial_product.8), channel_id=1, source_target_pairs={{0,1},{1,0},{2,3},{3,2},{4,5},{5,4},{6,7},{7,6},{8,9},{9,8},{10,11... | collective-permute-start | bytes 786440 | tf_op jit(solution)/shard_map/ppermute | solution.py:381
  57.7 22.4 %collective-permute-start.16 = (bf16[128,1024]{1,0:T(8,128)(2,1)S(1)}, bf16[128,1024]{1,0:T(8,128)(2,1)S(1)}, u32[]{:S(2)}, u32[]{:S(2)}) collective-permute-start(bf16[128,1024]{1,0:T(8,128)(2,1)S(1)} %copy-done.8), channel_id=1, source_target_pairs={{0,2},{1,3},{2,0},{3,1},{4,6},{5,7},{6,4},{7,5},{8,10},{9,11},{10,... | collective-permute-start | bytes 786440 | tf_op jit(solution)/shard_map/ppermute | solution.py:381
  58.8 3.4 %copy-start = (bf16[4096,1024]{1,0:T(8,128)(2,1)S(1)}, bf16[4096,1024]{1,0:T(8,128)(2,1)}, u32[]{:S(2)}) copy-start(bf16[4096,1024]{1,0:T(8,128)(2,1)} %refs_3_.15) | copy-start | bytes 25165828
  62.2 6.7 %copy-start.9 = (bf16[128,1024]{1,0:T(8,128)(2,1)S(1)}, bf16[128,1024]{1,0:T(8,128)(2,1)}, u32[]{:S(2)}) copy-start(bf16[128,1024]{1,0:T(8,128)(2,1)} %get-tuple-element.61.x_ref.refs_0_) | copy-start | bytes 786436
  63.4 6.8 %copy-start.7 = (bf16[128,1024]{1,0:T(8,128)(2,1)S(1)}, bf16[128,1024]{1,0:T(8,128)(2,1)}, u32[]{:S(2)}) copy-start(bf16[128,1024]{1,0:T(8,128)(2,1)} %get-tuple-element.66.x_ref.refs_0_) | copy-start | bytes 786436
  68.8 14.4 %copy-start.1 = (bf16[4096,1024]{1,0:T(8,128)(2,1)S(1)}, bf16[4096,1024]{1,0:T(8,128)(2,1)}, u32[]{:S(2)}) copy-start(bf16[4096,1024]{1,0:T(8,128)(2,1)} %refs_3_.15) | copy-start | bytes 25165828
  70.1 14.5 %collective-permute-start.15 = (bf16[128,1024]{1,0:T(8,128)(2,1)S(1)}, bf16[128,1024]{1,0:T(8,128)(2,1)S(1)}, u32[]{:S(2)}, u32[]{:S(2)}) collective-permute-start(bf16[128,1024]{1,0:T(8,128)(2,1)S(1)} %partial_product.9), channel_id=1, source_target_pairs={{0,1},{1,0},{2,3},{3,2},{4,5},{5,4},{6,7},{7,6},{8,9},{9,8},{10,11... | collective-permute-start | bytes 786440 | tf_op jit(solution)/shard_map/ppermute | solution.py:381
  70.2 11.2 %copy-start.6 = (bf16[128,1024]{1,0:T(8,128)(2,1)S(1)}, bf16[128,1024]{1,0:T(8,128)(2,1)}, u32[]{:S(2)}) copy-start(bf16[128,1024]{1,0:T(8,128)(2,1)} %get-tuple-element.72.x_ref.refs_0_) | copy-start | bytes 786436
  70.3 26.7 %collective-permute-start.14 = (bf16[128,1024]{1,0:T(8,128)(2,1)S(1)}, bf16[128,1024]{1,0:T(8,128)(2,1)S(1)}, u32[]{:S(2)}, u32[]{:S(2)}) collective-permute-start(bf16[128,1024]{1,0:T(8,128)(2,1)S(1)} %copy-done.7), channel_id=1, source_target_pairs={{0,2},{1,3},{2,0},{3,1},{4,6},{5,7},{6,4},{7,5},{8,10},{9,11},{10,... | collective-permute-start | bytes 786440 | tf_op jit(solution)/shard_map/ppermute | solution.py:381
  81.4 26.8 %collective-permute-start.19 = (bf16[128,1024]{1,0:T(8,128)(2,1)S(1)}, bf16[128,1024]{1,0:T(8,128)(2,1)S(1)}, u32[]{:S(2)}, u32[]{:S(2)}) collective-permute-start(bf16[128,1024]{1,0:T(8,128)(2,1)S(1)} %copy-done.6), channel_id=1, source_target_pairs={{0,2},{1,3},{2,0},{3,1},{4,6},{5,7},{6,4},{7,5},{8,10},{9,11},{10,... | collective-permute-start | bytes 786440 | tf_op jit(solution)/shard_map/ppermute | solution.py:381
  81.5 26.8 %collective-permute-start.20 = (bf16[128,1024]{1,0:T(8,128)(2,1)S(1)}, bf16[128,1024]{1,0:T(8,128)(2,1)S(1)}, u32[]{:S(2)}, u32[]{:S(2)}) collective-permute-start(bf16[128,1024]{1,0:T(8,128)(2,1)S(1)} %partial_product.10), channel_id=1, source_target_pairs={{0,1},{1,0},{2,3},{3,2},{4,5},{5,4},{6,7},{7,6},{8,9},{9,8},{10,11... | collective-permute-start | bytes 786440 | tf_op jit(solution)/shard_map/ppermute | solution.py:381
  84.6 13.6 %copy-start.5 = (bf16[128,1024]{1,0:T(8,128)(2,1)S(1)}, bf16[128,1024]{1,0:T(8,128)(2,1)}, u32[]{:S(2)}) copy-start(bf16[128,1024]{1,0:T(8,128)(2,1)} %get-tuple-element.70.x_ref.refs_0_) | copy-start | bytes 786436
  98.2 15.7 %collective-permute-start.17 = (bf16[128,1024]{1,0:T(8,128)(2,1)S(1)}, bf16[128,1024]{1,0:T(8,128)(2,1)S(1)}, u32[]{:S(2)}, u32[]{:S(2)}) collective-permute-start(bf16[128,1024]{1,0:T(8,128)(2,1)S(1)} %copy-done.5), channel_id=1, source_target_pairs={{0,2},{1,3},{2,0},{3,1},{4,6},{5,7},{6,4},{7,5},{8,10},{9,11},{10,... | collective-permute-start | bytes 786440 | tf_op jit(solution)/shard_map/ppermute | solution.py:381
  98.3 18.2 %collective-permute-start.18 = (bf16[128,1024]{1,0:T(8,128)(2,1)S(1)}, bf16[128,1024]{1,0:T(8,128)(2,1)S(1)}, u32[]{:S(2)}, u32[]{:S(2)}) collective-permute-start(bf16[128,1024]{1,0:T(8,128)(2,1)S(1)} %partial_product.11), channel_id=1, source_target_pairs={{0,1},{1,0},{2,3},{3,2},{4,5},{5,4},{6,7},{7,6},{8,9},{9,8},{10,11... | collective-permute-start | bytes 786440 | tf_op jit(solution)/shard_map/ppermute | solution.py:381
  101.0 8.6 %copy-start.4 = (bf16[128,1024]{1,0:T(8,128)(2,1)S(1)}, bf16[128,1024]{1,0:T(8,128)(2,1)}, u32[]{:S(2)}) copy-start(bf16[128,1024]{1,0:T(8,128)(2,1)} %get-tuple-element.81.x_ref.refs_0_) | copy-start | bytes 786436
  109.5 18.1 %collective-permute-start.24 = (bf16[128,1024]{1,0:T(8,128)(2,1)S(1)}, bf16[128,1024]{1,0:T(8,128)(2,1)S(1)}, u32[]{:S(2)}, u32[]{:S(2)}) collective-permute-start(bf16[128,1024]{1,0:T(8,128)(2,1)S(1)} %partial_product.12), channel_id=1, source_target_pairs={{0,1},{1,0},{2,3},{3,2},{4,5},{5,4},{6,7},{7,6},{8,9},{9,8},{10,11... | collective-permute-start | bytes 786440 | tf_op jit(solution)/shard_map/ppermute | solution.py:381
  109.6 18.0 %collective-permute-start.23 = (bf16[128,1024]{1,0:T(8,128)(2,1)S(1)}, bf16[128,1024]{1,0:T(8,128)(2,1)S(1)}, u32[]{:S(2)}, u32[]{:S(2)}) collective-permute-start(bf16[128,1024]{1,0:T(8,128)(2,1)S(1)} %copy-done.4), channel_id=1, source_target_pairs={{0,2},{1,3},{2,0},{3,1},{4,6},{5,7},{6,4},{7,5},{8,10},{9,11},{10,... | collective-permute-start | bytes 786440 | tf_op jit(solution)/shard_map/ppermute | solution.py:381
  117.7 17.0 %collective-permute-start.22 = (bf16[128,1024]{1,0:T(8,128)(2,1)S(1)}, bf16[128,1024]{1,0:T(8,128)(2,1)S(1)}, u32[]{:S(2)}, u32[]{:S(2)}) collective-permute-start(bf16[128,1024]{1,0:T(8,128)(2,1)S(1)} %partial_product.13), channel_id=1, source_target_pairs={{0,1},{1,0},{2,3},{3,2},{4,5},{5,4},{6,7},{7,6},{8,9},{9,8},{10,11... | collective-permute-start | bytes 786440 | tf_op jit(solution)/shard_map/ppermute | solution.py:381
  119.3 0.9 copy-start.3
  120.3 15.8 %collective-permute-start.21 = (bf16[128,1024]{1,0:T(8,128)(2,1)S(1)}, bf16[128,1024]{1,0:T(8,128)(2,1)S(1)}, u32[]{:S(2)}, u32[]{:S(2)}) collective-permute-start(bf16[128,1024]{1,0:T(8,128)(2,1)S(1)} %copy-done.3), channel_id=1, source_target_pairs={{0,2},{1,3},{2,0},{3,1},{4,6},{5,7},{6,4},{7,5},{8,10},{9,11},{10,... | collective-permute-start | bytes 786440 | tf_op jit(solution)/shard_map/ppermute | solution.py:381
  128.9 13.3 %collective-permute-start.26 = (bf16[128,1024]{1,0:T(8,128)(2,1)S(1)}, bf16[128,1024]{1,0:T(8,128)(2,1)S(1)}, u32[]{:S(2)}, u32[]{:S(2)}) collective-permute-start(bf16[128,1024]{1,0:T(8,128)(2,1)S(1)} %partial_product.14), channel_id=1, source_target_pairs={{0,1},{1,0},{2,3},{3,2},{4,5},{5,4},{6,7},{7,6},{8,9},{9,8},{10,11... | collective-permute-start | bytes 786440 | tf_op jit(solution)/shard_map/ppermute | solution.py:381
  137.3 10.0 %collective-permute-start.25 = (bf16[128,1024]{1,0:T(8,128)(2,1)S(1)}, bf16[128,1024]{1,0:T(8,128)(2,1)S(1)}, u32[]{:S(2)}, u32[]{:S(2)}) collective-permute-start(bf16[128,1024]{1,0:T(8,128)(2,1)S(1)} %partial_product.15), channel_id=1, source_target_pairs={{0,1},{1,0},{2,3},{3,2},{4,5},{5,4},{6,7},{7,6},{8,9},{9,8},{10,11... | collective-permute-start | bytes 786440 | tf_op jit(solution)/shard_map/ppermute | solution.py:381
where the time goes:
time: 148 us
  waiting for transfers between devices  62.1 us (42%)
  Pallas kernels  52.2 us (35%)
  starting transfers between devices  28.4 us (19%)
  local copies, waits for them, and re-layouts  3.69 us (2%)
    ppermute x24, waiting for transfers between devices, swap(): lax.ppermute(value, axis, [(i, i ^ distance) for i in range(lax.axis_size...  62.1 us
    ppermute x24, starting transfers between devices, swap(): lax.ppermute(value, axis, [(i, i ^ distance) for i in range(lax.axis_size...  20.1 us
    pallas_call x8, Pallas kernels, project(): pl.pallas_call(functools.partial(project_kernel, sources), grid_spec=pltp...  10.3 us
    pallas_call x8, Pallas kernels, partial_product(): pl.pallas_call(partial_kernel, grid_spec=pltpu.PrefetchScalarGridSpec(num...  10.2 us
    pallas_call x1, Pallas kernels, query_side(): pl.pallas_call(query_kernel, grid=(heads // group,), in_specs=[pl.BlockSp...  9.8 us
    ppermute x3, starting transfers between devices, earlier_states(): theirs = lax.ppermute(total, 'ctx', pairs)  8.25 us
    pallas_call x1, Pallas kernels, key_side(): pl.pallas_call(functools.partial(key_kernel, weight is not None), grid_sp...  8.16 us
    pallas_call x2, Pallas kernels, finish(): pl.pallas_call(functools.partial(finish_kernel, group, span, cuts), grid_...  7.65 us
  transfers between devices with their start and end apart: 27, of which 16 were waited for; matrix products, arithmetic and copies ran while one was open for 1% of the time, Pallas kernels for 29%

commit v1 on v0

--- a/solution.py
+++ b/solution.py
@@ -137,7 +137,7 @@
             num_scalar_prefetch=3, grid=(steps,), in_specs=in_specs, out_specs=out_specs
         ),
         out_shape=out_shape,
-        compiler_params=LARGE,
+        compiler_params=pltpu.CompilerParams(vmem_limit_bytes=53 << 20),
         cost_estimate=FREE,
         name="key_side",
     )(core, place, turn, *operands)
@@ -201,7 +201,7 @@
             jax.ShapeDtypeStruct((heads, rows, 2 * count), BF16),
             jax.ShapeDtypeStruct((rows, heads * width), BF16),
         ],
-        compiler_params=LARGE,
+        compiler_params=MIDDLE,
         cost_estimate=FREE,
         name="query_side",
     )(query_rows, value_rows, frequencies, key_feat)
@@ -288,7 +288,7 @@
 def project(blocks, weight, place, hops, dtype=BF16):
     size, depth = blocks[0].shape
     cols = weight.shape[1]
-    step = min(512, cols)
+    step = min(1024, cols)
 
     def rows_of(source):
         return lambda n, p: (p[0] ^ hops[source], n)
@@ -333,7 +333,7 @@
 def partial_product(core, turn, blocks, weights):
     size, depth = blocks[0].shape
     cols = weights[0].shape[1]
-    step = min(512, cols)
+    step = min(1024, cols)
     return pl.pallas_call(
         partial_kernel,
         grid_spec=pltpu.PrefetchScalarGridSpec(

time: 148 us -> 148 us (level)
  Pallas kernels: 52.2 us -> 43.2 us
  waiting for transfers between devices: 62.1 us -> 67.5 us
  starting transfers between devices: 28.4 us -> 31.7 us
    ppermute x24, waiting for transfers between devices: 62.1 us -> 67.4 us  [swap(): lax.ppermute(value, axis, [(i, i ^ distance) for i in range(lax.axis_size...]
    pallas_call x8, Pallas kernels: 10.3 us -> 5.87 us  [project(): pl.pallas_call(functools.partial(project_kernel, sources), grid_spec=pltp...]
    pallas_call x8, Pallas kernels: 10.2 us -> 5.84 us  [partial_product(): pl.pallas_call(partial_kernel, grid_spec=pltpu.PrefetchScalarGridSpec(num...]
    ppermute x24, starting transfers between devices: 20.1 us -> 23.5 us  [swap(): lax.ppermute(value, axis, [(i, i ^ distance) for i in range(lax.axis_size...]
    unnamed x26 -> x28, local copies, waits for them, and re-layouts: 3.62 us -> 4.57 us
  transfers between devices with their start and end apart: 27 -> 27, of which waited for: 16 -> 17; matrix products, arithmetic and copies ran while one was open for 1% -> 0% of each run, Pallas kernels for 29% -> 23%
where the time goes in v1:
time: 148 us
  waiting for transfers between devices  67.5 us (46%)
  Pallas kernels  43.2 us (29%)
  starting transfers between devices  31.7 us (21%)
  local copies, waits for them, and re-layouts  4.63 us (3%)
    ppermute x24, waiting for transfers between devices, swap(): lax.ppermute(value, axis, [(i, i ^ distance) for i in range(lax.axis_size...  67.4 us
    ppermute x24, starting transfers between devices, swap(): lax.ppermute(value, axis, [(i, i ^ distance) for i in range(lax.axis_size...  23.5 us
    pallas_call x1, Pallas kernels, query_side(): pl.pallas_call(query_kernel, grid=(heads // group,), in_specs=[pl.BlockSp...  9.73 us
    ppermute x3, starting transfers between devices, earlier_states(): theirs = lax.ppermute(total, 'ctx', pairs)  8.16 us
    pallas_call x1, Pallas kernels, key_side(): pl.pallas_call(functools.partial(key_kernel, weight is not None), grid_sp...  8.06 us
    pallas_call x2, Pallas kernels, finish(): pl.pallas_call(functools.partial(finish_kernel, group, span, cuts), grid_...  7.65 us
    pallas_call x8, Pallas kernels, join(): pl.pallas_call(join_kernel, grid=(size // step,), in_specs=[spec, spec] +...  6.05 us
    pallas_call x8, Pallas kernels, project(): pl.pallas_call(functools.partial(project_kernel, sources), grid_spec=pltp...  5.87 us
  transfers between devices with their start and end apart: 27, of which 17 were waited for; matrix products, arithmetic and copies ran while one was open for 0% of the time, Pallas kernels for 23%

profile of v1, /device:TPU:0, one launch (start us, length us, event | category | flops | bytes accessed | tf_op | source)
XLA Modules:
  0.0 147.8 jit_solution(9788775404478681850)
XLA Ops:
  0.0 0.9 copy-done.11
  1.0 8.1 %key_side.1 = (bf16[8,256,1024]{2,1,0:T(8,128)(2,1)}, bf16[4,256,128]{2,1,0:T(8,128)(2,1)S(1)}, bf16[4,256,128]{2,1,0:T(8,128)(2,1)S(1)}, f32[8,1,256,128]{3,2,1,0:T(8,128)}, bf16[512,1024]{1,0:T(8,128)(2,1)}) custom-call(s32[1]{0:T(128)} %bitcast.1.core_ref, s32[1]{0:T(128)} %bitcast.place_ref, s32[1]{0:T(128)} %bitcast.2.turn_ref, ...), custom_call_target="tpu_custom_call" | custom-call | tf_op jit(solution)/shard_map/key_side/pallas_call | solution.py:134
  9.5 2.5 %collective-permute-start.1 = (bf16[512,1024]{1,0:T(8,128)(2,1)}, bf16[512,1024]{1,0:T(8,128)(2,1)S(1)}, u32[]{:S(2)}, u32[]{:S(2)}) collective-permute-start(bf16[512,1024]{1,0:T(8,128)(2,1)} %get-tuple-element.50), channel_id=1, source_target_pairs={{0,1},{1,0},{2,3},{3,2},{4,5},{5,4},{6,7},{7,6},{8,9},{9,8},{10,11... | collective-permute-start | bytes 3145736 | tf_op jit(solution)/shard_map/ppermute | solution.py:381
  12.1 3.4 %collective-permute-start.2 = (bf16[4,256,128]{2,1,0:T(8,128)(2,1)S(1)}, bf16[4,256,128]{2,1,0:T(8,128)(2,1)S(1)}, u32[]{:S(2)}, u32[]{:S(2)}) collective-permute-start(bf16[4,256,128]{2,1,0:T(8,128)(2,1)S(1)} %fusion.2), channel_id=1, source_target_pairs={{0,8},{4,12},{16,24},{20,28},{1,9},{5,13},{17,25},{21,29},{2,10},{... | collective-permute-start | bytes 786440 | tf_op jit(solution)/shard_map/ppermute | solution.py:399
  15.6 3.4 %collective-permute-start.3 = (bf16[4,256,128]{2,1,0:T(8,128)(2,1)S(1)}, bf16[4,256,128]{2,1,0:T(8,128)(2,1)S(1)}, u32[]{:S(2)}, u32[]{:S(2)}) collective-permute-start(bf16[4,256,128]{2,1,0:T(8,128)(2,1)S(1)} %fusion.2), channel_id=1, source_target_pairs={{0,16},{4,20},{8,24},{12,28},{1,17},{5,21},{9,25},{13,29},{2,18},{... | collective-permute-start | bytes 786440 | tf_op jit(solution)/shard_map/ppermute | solution.py:399
  19.0 1.3 collective-permute-start.4
  20.4 9.7 %query_side.1 = (bf16[8,1024,256]{2,1,0:T(8,128)(2,1)}, bf16[1024,1024]{1,0:T(8,128)(2,1)}) custom-call(bf16[1024,1024]{1,0:T(8,128)(2,1)} %query_ref.1, bf16[1024,1024]{1,0:T(8,128)(2,1)} %value_ref.3, bf16[8,128,128]{2,1,0:T(8,128)(2,1)S(1)} %copy-done.12, bf16[8,256,1024]{2,1,0:T(8,128)(2,1)} %get-tuple-element.48.key_feat_ref), custom_call_target="tpu_custom_call" | custom-call | tf_op jit(solution)/shard_map/query_side/pallas_call | solution.py:187
  30.6 1.5 %collective-permute-done.5.theirs_ref = bf16[4,256,128]{2,1,0:T(8,128)(2,1)S(1)} collective-permute-done((bf16[4,256,128]{2,1,0:T(8,128)(2,1)S(1)}, bf16[4,256,128]{2,1,0:T(8,128)(2,1)S(1)}, u32[]{:S(2)}, u32[]{:S(2)}) %collective-permute-start.5) | collective-permute-done | bytes 262176 | tf_op jit(solution)/shard_map/ppermute | solution.py:381
  32.1 1.8 %finish.2.x_ref.refs_0_ = bf16[128,1024]{1,0:T(8,128)(2,1)S(1)} custom-call(s32[1]{0:T(128)} %bitcast.1.core_ref, bf16[8,1024,256]{2,1,0:T(8,128)(2,1)} %get-tuple-element.56.feat_ref, bf16[1024,1024]{1,0:T(8,128)(2,1)} %get-tuple-element.51.local_ref, bf16[4,256,128]{2,1,0:T(8,128)(2,1)S(1)} %collective-permute-done.5.theirs_ref, ...), custom_call_target="tpu_custom_call" | custom-call | tf_op jit(solution)/shard_map/finish/pallas_call | solution.py:262
  34.0 2.6 %collective-permute-start.7 = (bf16[128,1024]{1,0:T(8,128)(2,1)S(1)}, bf16[128,1024]{1,0:T(8,128)(2,1)S(1)}, u32[]{:S(2)}, u32[]{:S(2)}) collective-permute-start(bf16[128,1024]{1,0:T(8,128)(2,1)S(1)} %finish.2.x_ref.refs_0_), channel_id=1, source_target_pairs={{0,2},{1,3},{2,0},{3,1},{4,6},{5,7},{6,4},{7,5},{8,10},{9,11},{10,... | collective-permute-start | bytes 786440 | tf_op jit(solution)/shard_map/ppermute | solution.py:381
  36.7 2.6 %collective-permute-start.9 = (bf16[256,1024]{1,0:T(8,128)(2,1)S(1)}, bf16[256,1024]{1,0:T(8,128)(2,1)S(1)}, u32[]{:S(2)}, u32[]{:S(2)}) collective-permute-start(bf16[256,1024]{1,0:T(8,128)(2,1)S(1)} %get-tuple-element.85), channel_id=1, source_target_pairs={{0,16},{4,20},{8,24},{12,28},{16,0},{20,4},{24,8},{28,12},{1,17},{... | collective-permute-start | bytes 1572872 | tf_op jit(solution)/shard_map/ppermute | solution.py:381
  39.4 5.8 %finish.3 = (bf16[128,1024]{1,0:T(8,128)(2,1)}, bf16[128,1024]{1,0:T(8,128)(2,1)}, bf16[128,1024]{1,0:T(8,128)(2,1)}, bf16[128,1024]{1,0:T(8,128)(2,1)}, bf16[12...) custom-call(s32[1]{0:T(128)} %bitcast.1.core_ref, ...), custom_call_target="tpu_custom_call" | custom-call | tf_op jit(solution)/shard_map/finish/pallas_call | solution.py:262
  45.2 3.7 %collective-permute-done.7.y_ref.refs_1_ = bf16[128,1024]{1,0:T(8,128)(2,1)S(1)} collective-permute-done((bf16[128,1024]{1,0:T(8,128)(2,1)S(1)}, bf16[128,1024]{1,0:T(8,128)(2,1)S(1)}, u32[]{:S(2)}, u32[]{:S(2)}) %collective-permute-start.7) | collective-permute-done | bytes 262176 | tf_op jit(solution)/shard_map/ppermute | solution.py:381
  48.9 2.3 %collective-permute-done.9.refs_2_ = bf16[256,1024]{1,0:T(8,128)(2,1)S(1)} collective-permute-done((bf16[256,1024]{1,0:T(8,128)(2,1)S(1)}, bf16[256,1024]{1,0:T(8,128)(2,1)S(1)}, u32[]{:S(2)}, u32[]{:S(2)}) %collective-permute-start.9) | collective-permute-done | bytes 524320 | tf_op jit(solution)/shard_map/ppermute | solution.py:381
  51.2 1.5 collective-permute-done.8.refs_1_
  52.7 1.1 collective-permute-start.6
  53.8 0.8 collective-permute-done.11.refs_4_
  55.3 1.5 %collective-permute-start.13 = (bf16[128,1024]{1,0:T(8,128)(2,1)S(1)}, bf16[128,1024]{1,0:T(8,128)(2,1)S(1)}, u32[]{:S(2)}, u32[]{:S(2)}) collective-permute-start(bf16[128,1024]{1,0:T(8,128)(2,1)S(1)} %partial_product.8), channel_id=1, source_target_pairs={{0,1},{1,0},{2,3},{3,2},{4,5},{5,4},{6,7},{7,6},{8,9},{9,8},{10,11... | collective-permute-start | bytes 786440 | tf_op jit(solution)/shard_map/ppermute | solution.py:381
  56.8 1.2 collective-permute-start.16
  58.0 3.4 %copy-done = bf16[4096,1024]{1,0:T(8,128)(2,1)S(1)} copy-done((bf16[4096,1024]{1,0:T(8,128)(2,1)S(1)}, bf16[4096,1024]{1,0:T(8,128)(2,1)}, u32[]{:S(2)}) %copy-start) | copy-done | bytes 8388632
  62.2 6.4 %collective-permute-done.6.y_ref.refs_1_ = bf16[128,1024]{1,0:T(8,128)(2,1)S(1)} collective-permute-done((bf16[128,1024]{1,0:T(8,128)(2,1)}, bf16[128,1024]{1,0:T(8,128)(2,1)S(1)}, u32[]{:S(2)}, u32[]{:S(2)}) %collective-permute-start.6) | collective-permute-done | bytes 262176 | tf_op jit(solution)/shard_map/ppermute | solution.py:381
  69.5 2.6 %collective-permute-start.14 = (bf16[128,1024]{1,0:T(8,128)(2,1)S(1)}, bf16[128,1024]{1,0:T(8,128)(2,1)S(1)}, u32[]{:S(2)}, u32[]{:S(2)}) collective-permute-start(bf16[128,1024]{1,0:T(8,128)(2,1)S(1)} %copy-done.7), channel_id=1, source_target_pairs={{0,2},{1,3},{2,0},{3,1},{4,6},{5,7},{6,4},{7,5},{8,10},{9,11},{10,... | collective-permute-start | bytes 786440 | tf_op jit(solution)/shard_map/ppermute | solution.py:381
  72.0 7.9 %collective-permute-done.16.y_ref.refs_1_ = bf16[128,1024]{1,0:T(8,128)(2,1)S(1)} collective-permute-done((bf16[128,1024]{1,0:T(8,128)(2,1)S(1)}, bf16[128,1024]{1,0:T(8,128)(2,1)S(1)}, u32[]{:S(2)}, u32[]{:S(2)}) %collective-permute-start.16) | collective-permute-done | bytes 262176 | tf_op jit(solution)/shard_map/ppermute | solution.py:381
  80.7 2.5 %collective-permute-start.20 = (bf16[128,1024]{1,0:T(8,128)(2,1)S(1)}, bf16[128,1024]{1,0:T(8,128)(2,1)S(1)}, u32[]{:S(2)}, u32[]{:S(2)}) collective-permute-start(bf16[128,1024]{1,0:T(8,128)(2,1)S(1)} %partial_product.10), channel_id=1, source_target_pairs={{0,1},{1,0},{2,3},{3,2},{4,5},{5,4},{6,7},{7,6},{8,9},{9,8},{10,11... | collective-permute-start | bytes 786440 | tf_op jit(solution)/shard_map/ppermute | solution.py:381
  84.0 12.7 %collective-permute-done.14.y_ref.refs_1_ = bf16[128,1024]{1,0:T(8,128)(2,1)S(1)} collective-permute-done((bf16[128,1024]{1,0:T(8,128)(2,1)S(1)}, bf16[128,1024]{1,0:T(8,128)(2,1)S(1)}, u32[]{:S(2)}, u32[]{:S(2)}) %collective-permute-start.14) | collective-permute-done | bytes 262176 | tf_op jit(solution)/shard_map/ppermute | solution.py:381
  97.5 2.2 %collective-permute-start.18 = (bf16[128,1024]{1,0:T(8,128)(2,1)S(1)}, bf16[128,1024]{1,0:T(8,128)(2,1)S(1)}, u32[]{:S(2)}, u32[]{:S(2)}) collective-permute-start(bf16[128,1024]{1,0:T(8,128)(2,1)S(1)} %partial_product.11), channel_id=1, source_target_pairs={{0,1},{1,0},{2,3},{3,2},{4,5},{5,4},{6,7},{7,6},{8,9},{9,8},{10,11... | collective-permute-start | bytes 786440 | tf_op jit(solution)/shard_map/ppermute | solution.py:381
  99.7 0.7 project.11.a_ref
  100.5 7.6 %collective-permute-done.19.y_ref.refs_1_ = bf16[128,1024]{1,0:T(8,128)(2,1)S(1)} collective-permute-done((bf16[128,1024]{1,0:T(8,128)(2,1)S(1)}, bf16[128,1024]{1,0:T(8,128)(2,1)S(1)}, u32[]{:S(2)}, u32[]{:S(2)}) %collective-permute-start.19) | collective-permute-done | bytes 262176 | tf_op jit(solution)/shard_map/ppermute | solution.py:381
  108.0 0.7 partial_product.12
  108.9 2.2 %collective-permute-start.23 = (bf16[128,1024]{1,0:T(8,128)(2,1)S(1)}, bf16[128,1024]{1,0:T(8,128)(2,1)S(1)}, u32[]{:S(2)}, u32[]{:S(2)}) collective-permute-start(bf16[128,1024]{1,0:T(8,128)(2,1)S(1)} %copy-done.4), channel_id=1, source_target_pairs={{0,2},{1,3},{2,0},{3,1},{4,6},{5,7},{6,4},{7,5},{8,10},{9,11},{10,... | collective-permute-start | bytes 786440 | tf_op jit(solution)/shard_map/ppermute | solution.py:381
  111.8 1.9 %collective-permute-done.17.y_ref.refs_1_ = bf16[128,1024]{1,0:T(8,128)(2,1)S(1)} collective-permute-done((bf16[128,1024]{1,0:T(8,128)(2,1)S(1)}, bf16[128,1024]{1,0:T(8,128)(2,1)S(1)}, u32[]{:S(2)}, u32[]{:S(2)}) %collective-permute-start.17) | collective-permute-done | bytes 262176 | tf_op jit(solution)/shard_map/ppermute | solution.py:381
  113.6 2.9 %collective-permute-done.18.b_ref = bf16[128,1024]{1,0:T(8,128)(2,1)S(1)} collective-permute-done((bf16[128,1024]{1,0:T(8,128)(2,1)S(1)}, bf16[128,1024]{1,0:T(8,128)(2,1)S(1)}, u32[]{:S(2)}, u32[]{:S(2)}) %collective-permute-start.18) | collective-permute-done | bytes 262176 | tf_op jit(solution)/shard_map/ppermute | solution.py:381
  116.5 0.7 partial_product.13
  117.3 0.8 join.8.refs_0_
  118.1 0.7 join.9.refs_0_
  118.9 0.8 join.10.refs_0_
  119.8 1.4 collective-permute-start.21
  121.9 5.8 %collective-permute-done.24.b_ref = bf16[128,1024]{1,0:T(8,128)(2,1)S(1)} collective-permute-done((bf16[128,1024]{1,0:T(8,128)(2,1)S(1)}, bf16[128,1024]{1,0:T(8,128)(2,1)S(1)}, u32[]{:S(2)}, u32[]{:S(2)}) %collective-permute-start.24) | collective-permute-done | bytes 262176 | tf_op jit(solution)/shard_map/ppermute | solution.py:381
  129.3 5.4 %collective-permute-done.22.b_ref = bf16[128,1024]{1,0:T(8,128)(2,1)S(1)} collective-permute-done((bf16[128,1024]{1,0:T(8,128)(2,1)S(1)}, bf16[128,1024]{1,0:T(8,128)(2,1)S(1)}, u32[]{:S(2)}, u32[]{:S(2)}) %collective-permute-start.22) | collective-permute-done | bytes 262176 | tf_op jit(solution)/shard_map/ppermute | solution.py:381
  134.6 1.2 collective-permute-done.21.refs_1_.y_ref
  136.6 0.7 project.15.a_ref
  137.4 0.8 join.11.refs_0_
  138.1 0.7 join.12.refs_0_
  139.6 0.8 join.13.refs_0_
  140.4 1.0 collective-permute-done.26.b_ref
  141.4 0.7 join.14.refs_0_
  142.2 4.9 %collective-permute-done.25.b_ref = bf16[128,1024]{1,0:T(8,128)(2,1)S(1)} collective-permute-done((bf16[128,1024]{1,0:T(8,128)(2,1)S(1)}, bf16[128,1024]{1,0:T(8,128)(2,1)S(1)}, u32[]{:S(2)}, u32[]{:S(2)}) %collective-permute-start.25) | collective-permute-done | bytes 262176 | tf_op jit(solution)/shard_map/ppermute | solution.py:381
  147.0 0.8 join.15
  (65 shorter events, 10.8 us)
Async XLA Ops:
  0.0 0.9 copy-start.11
  1.0 19.4 %copy-start.12 = (bf16[8,128,128]{2,1,0:T(8,128)(2,1)S(1)}, bf16[8,128,128]{2,1,0:T(8,128)(2,1)}, u32[]{:S(2)}) copy-start(bf16[8,128,128]{2,1,0:T(8,128)(2,1)} %freq_ref.2) | copy-start | bytes 786436
  9.0 3.0 %collective-permute-start = (bf16[4,256,128]{2,1,0:T(8,128)(2,1)S(1)}, bf16[4,256,128]{2,1,0:T(8,128)(2,1)S(1)}, u32[]{:S(2)}, u32[]{:S(2)}) collective-permute-start(bf16[4,256,128]{2,1,0:T(8,128)(2,1)S(1)} %get-tuple-element.46), channel_id=1, source_target_pairs={{0,4},{4,0},{8,12},{12,8},{16,20},{20,16},{24,28},{28,24},{1,5},{5... | collective-permute-start | bytes 786440 | tf_op jit(solution)/shard_map/ppermute | solution.py:381
  9.5 27.1 %collective-permute-start.1 = (bf16[512,1024]{1,0:T(8,128)(2,1)}, bf16[512,1024]{1,0:T(8,128)(2,1)S(1)}, u32[]{:S(2)}, u32[]{:S(2)}) collective-permute-start(bf16[512,1024]{1,0:T(8,128)(2,1)} %get-tuple-element.50), channel_id=1, source_target_pairs={{0,1},{1,0},{2,3},{3,2},{4,5},{5,4},{6,7},{7,6},{8,9},{9,8},{10,11... | collective-permute-start | bytes 3145736 | tf_op jit(solution)/shard_map/ppermute | solution.py:381
  12.1 18.0 %collective-permute-start.2 = (bf16[4,256,128]{2,1,0:T(8,128)(2,1)S(1)}, bf16[4,256,128]{2,1,0:T(8,128)(2,1)S(1)}, u32[]{:S(2)}, u32[]{:S(2)}) collective-permute-start(bf16[4,256,128]{2,1,0:T(8,128)(2,1)S(1)} %fusion.2), channel_id=1, source_target_pairs={{0,8},{4,12},{16,24},{20,28},{1,9},{5,13},{17,25},{21,29},{2,10},{... | collective-permute-start | bytes 786440 | tf_op jit(solution)/shard_map/ppermute | solution.py:399
  15.6 14.7 %collective-permute-start.3 = (bf16[4,256,128]{2,1,0:T(8,128)(2,1)S(1)}, bf16[4,256,128]{2,1,0:T(8,128)(2,1)S(1)}, u32[]{:S(2)}, u32[]{:S(2)}) collective-permute-start(bf16[4,256,128]{2,1,0:T(8,128)(2,1)S(1)} %fusion.2), channel_id=1, source_target_pairs={{0,16},{4,20},{8,24},{12,28},{1,17},{5,21},{9,25},{13,29},{2,18},{... | collective-permute-start | bytes 786440 | tf_op jit(solution)/shard_map/ppermute | solution.py:399
  19.0 11.2 %collective-permute-start.4 = (bf16[4,256,128]{2,1,0:T(8,128)(2,1)S(1)}, bf16[4,256,128]{2,1,0:T(8,128)(2,1)S(1)}, u32[]{:S(2)}, u32[]{:S(2)}) collective-permute-start(bf16[4,256,128]{2,1,0:T(8,128)(2,1)S(1)} %fusion.2), channel_id=1, source_target_pairs={{0,24},{4,28},{8,16},{12,20},{1,25},{5,29},{9,17},{13,21},{2,26},{... | collective-permute-start | bytes 786440 | tf_op jit(solution)/shard_map/ppermute | solution.py:399
  20.3 11.8 %copy-start.13 = (bf16[1024]{0:T(1024)(128)(2,1)S(1)}, bf16[1024]{0:T(1024)(128)(2,1)}, u32[]{:S(2)}) copy-start(bf16[1024]{0:T(1024)(128)(2,1)} %param.10) | copy-start | bytes 6148
  30.5 3.5 %copy-start.2 = (bf16[4,256,128]{2,1,0:T(8,128)(2,1)}, bf16[4,256,128]{2,1,0:T(8,128)(2,1)S(1)}, u32[]{:S(2)}) copy-start(bf16[4,256,128]{2,1,0:T(8,128)(2,1)S(1)} %get-tuple-element.87.mine_ref) | copy-start | bytes 786436
  30.5 1.6 %collective-permute-start.5 = (bf16[4,256,128]{2,1,0:T(8,128)(2,1)S(1)}, bf16[4,256,128]{2,1,0:T(8,128)(2,1)S(1)}, u32[]{:S(2)}, u32[]{:S(2)}) collective-permute-start(bf16[4,256,128]{2,1,0:T(8,128)(2,1)S(1)} %get-tuple-element.88), channel_id=1, source_target_pairs={{0,4},{4,0},{8,12},{12,8},{16,20},{20,16},{24,28},{28,24},{1,5},{5... | collective-permute-start | bytes 786440 | tf_op jit(solution)/shard_map/ppermute | solution.py:381
  32.1 1.8 %copy-start.10 = (bf16[4,256,128]{2,1,0:T(8,128)(2,1)}, bf16[4,256,128]{2,1,0:T(8,128)(2,1)S(1)}, u32[]{:S(2)}) copy-start(bf16[4,256,128]{2,1,0:T(8,128)(2,1)S(1)} %collective-permute-done.5.theirs_ref) | copy-start | bytes 786436
  34.0 14.9 %collective-permute-start.7 = (bf16[128,1024]{1,0:T(8,128)(2,1)S(1)}, bf16[128,1024]{1,0:T(8,128)(2,1)S(1)}, u32[]{:S(2)}, u32[]{:S(2)}) collective-permute-start(bf16[128,1024]{1,0:T(8,128)(2,1)S(1)} %finish.2.x_ref.refs_0_), channel_id=1, source_target_pairs={{0,2},{1,3},{2,0},{3,1},{4,6},{5,7},{6,4},{7,5},{8,10},{9,11},{10,... | collective-permute-start | bytes 786440 | tf_op jit(solution)/shard_map/ppermute | solution.py:381
  36.7 14.5 %collective-permute-start.9 = (bf16[256,1024]{1,0:T(8,128)(2,1)S(1)}, bf16[256,1024]{1,0:T(8,128)(2,1)S(1)}, u32[]{:S(2)}, u32[]{:S(2)}) collective-permute-start(bf16[256,1024]{1,0:T(8,128)(2,1)S(1)} %get-tuple-element.85), channel_id=1, source_target_pairs={{0,16},{4,20},{8,24},{12,28},{16,0},{20,4},{24,8},{28,12},{1,17},{... | collective-permute-start | bytes 1572872 | tf_op jit(solution)/shard_map/ppermute | solution.py:381
  39.3 13.4 %collective-permute-start.8 = (bf16[256,1024]{1,0:T(8,128)(2,1)S(1)}, bf16[256,1024]{1,0:T(8,128)(2,1)S(1)}, u32[]{:S(2)}, u32[]{:S(2)}) collective-permute-start(bf16[256,1024]{1,0:T(8,128)(2,1)S(1)} %get-tuple-element.86), channel_id=1, source_target_pairs={{0,8},{4,12},{8,0},{12,4},{16,24},{20,28},{24,16},{28,20},{1,9},{5... | collective-permute-start | bytes 1572872 | tf_op jit(solution)/shard_map/ppermute | solution.py:381
  48.9 5.7 %collective-permute-start.10 = (bf16[512,1024]{1,0:T(8,128)(2,1)S(1)}, bf16[512,1024]{1,0:T(8,128)(2,1)S(1)}, u32[]{:S(2)}, u32[]{:S(2)}) collective-permute-start(bf16[512,1024]{1,0:T(8,128)(2,1)S(1)} %collective-permute-done.1.refs_0_), channel_id=1, source_target_pairs={{0,4},{4,0},{8,12},{12,8},{16,20},{20,16},{24,28},{28,24},{1,5},{5... | collective-permute-start | bytes 3145736 | tf_op jit(solution)/shard_map/ppermute | solution.py:381
  51.2 2.5 %collective-permute-start.12 = (bf16[256,1024]{1,0:T(8,128)(2,1)S(1)}, bf16[256,1024]{1,0:T(8,128)(2,1)S(1)}, u32[]{:S(2)}, u32[]{:S(2)}) collective-permute-start(bf16[256,1024]{1,0:T(8,128)(2,1)S(1)} %collective-permute-done.9.refs_2_), channel_id=1, source_target_pairs={{0,4},{4,0},{8,12},{12,8},{16,20},{20,16},{24,28},{28,24},{1,5},{5... | collective-permute-start | bytes 1572872 | tf_op jit(solution)/shard_map/ppermute | solution.py:381
  52.7 1.9 %collective-permute-start.11 = (bf16[256,1024]{1,0:T(8,128)(2,1)S(1)}, bf16[256,1024]{1,0:T(8,128)(2,1)S(1)}, u32[]{:S(2)}, u32[]{:S(2)}) collective-permute-start(bf16[256,1024]{1,0:T(8,128)(2,1)S(1)} %collective-permute-done.8.refs_1_), channel_id=1, source_target_pairs={{0,4},{4,0},{8,12},{12,8},{16,20},{20,16},{24,28},{28,24},{1,5},{5... | collective-permute-start | bytes 1572872 | tf_op jit(solution)/shard_map/ppermute | solution.py:381
  52.7 4.2 %copy-start.8 = (bf16[128,1024]{1,0:T(8,128)(2,1)S(1)}, bf16[128,1024]{1,0:T(8,128)(2,1)}, u32[]{:S(2)}) copy-start(bf16[128,1024]{1,0:T(8,128)(2,1)} %get-tuple-element.67.x_ref.refs_0_) | copy-start | bytes 786436
  52.7 15.9 %collective-permute-start.6 = (bf16[128,1024]{1,0:T(8,128)(2,1)}, bf16[128,1024]{1,0:T(8,128)(2,1)S(1)}, u32[]{:S(2)}, u32[]{:S(2)}) collective-permute-start(bf16[128,1024]{1,0:T(8,128)(2,1)} %get-tuple-element.61.x_ref.refs_0_), channel_id=1, source_target_pairs={{0,2},{1,3},{2,0},{3,1},{4,6},{5,7},{6,4},{7,5},{8,10},{9,11},{10,... | collective-permute-start | bytes 786440 | tf_op jit(solution)/shard_map/ppermute | solution.py:381
  55.3 14.1 %collective-permute-start.13 = (bf16[128,1024]{1,0:T(8,128)(2,1)S(1)}, bf16[128,1024]{1,0:T(8,128)(2,1)S(1)}, u32[]{:S(2)}, u32[]{:S(2)}) collective-permute-start(bf16[128,1024]{1,0:T(8,128)(2,1)S(1)} %partial_product.8), channel_id=1, source_target_pairs={{0,1},{1,0},{2,3},{3,2},{4,5},{5,4},{6,7},{7,6},{8,9},{9,8},{10,11... | collective-permute-start | bytes 786440 | tf_op jit(solution)/shard_map/ppermute | solution.py:381
  56.8 23.1 %collective-permute-start.16 = (bf16[128,1024]{1,0:T(8,128)(2,1)S(1)}, bf16[128,1024]{1,0:T(8,128)(2,1)S(1)}, u32[]{:S(2)}, u32[]{:S(2)}) collective-permute-start(bf16[128,1024]{1,0:T(8,128)(2,1)S(1)} %copy-done.8), channel_id=1, source_target_pairs={{0,2},{1,3},{2,0},{3,1},{4,6},{5,7},{6,4},{7,5},{8,10},{9,11},{10,... | collective-permute-start | bytes 786440 | tf_op jit(solution)/shard_map/ppermute | solution.py:381
  58.0 3.4 %copy-start = (bf16[4096,1024]{1,0:T(8,128)(2,1)S(1)}, bf16[4096,1024]{1,0:T(8,128)(2,1)}, u32[]{:S(2)}) copy-start(bf16[4096,1024]{1,0:T(8,128)(2,1)} %refs_3_.15) | copy-start | bytes 25165828
  61.4 7.2 %copy-start.9 = (bf16[128,1024]{1,0:T(8,128)(2,1)S(1)}, bf16[128,1024]{1,0:T(8,128)(2,1)}, u32[]{:S(2)}) copy-start(bf16[128,1024]{1,0:T(8,128)(2,1)} %get-tuple-element.61.x_ref.refs_0_) | copy-start | bytes 786436
  62.2 7.3 %copy-start.7 = (bf16[128,1024]{1,0:T(8,128)(2,1)S(1)}, bf16[128,1024]{1,0:T(8,128)(2,1)}, u32[]{:S(2)}) copy-start(bf16[128,1024]{1,0:T(8,128)(2,1)} %get-tuple-element.66.x_ref.refs_0_) | copy-start | bytes 786436
  68.6 14.6 %copy-start.1 = (bf16[4096,1024]{1,0:T(8,128)(2,1)S(1)}, bf16[4096,1024]{1,0:T(8,128)(2,1)}, u32[]{:S(2)}) copy-start(bf16[4096,1024]{1,0:T(8,128)(2,1)} %refs_3_.15) | copy-start | bytes 25165828
  69.4 14.6 %collective-permute-start.15 = (bf16[128,1024]{1,0:T(8,128)(2,1)S(1)}, bf16[128,1024]{1,0:T(8,128)(2,1)S(1)}, u32[]{:S(2)}, u32[]{:S(2)}) collective-permute-start(bf16[128,1024]{1,0:T(8,128)(2,1)S(1)} %partial_product.9), channel_id=1, source_target_pairs={{0,1},{1,0},{2,3},{3,2},{4,5},{5,4},{6,7},{7,6},{8,9},{9,8},{10,11... | collective-permute-start | bytes 786440 | tf_op jit(solution)/shard_map/ppermute | solution.py:381
  69.5 11.2 %copy-start.6 = (bf16[128,1024]{1,0:T(8,128)(2,1)S(1)}, bf16[128,1024]{1,0:T(8,128)(2,1)}, u32[]{:S(2)}) copy-start(bf16[128,1024]{1,0:T(8,128)(2,1)} %get-tuple-element.72.x_ref.refs_0_) | copy-start | bytes 786436
  69.5 27.2 %collective-permute-start.14 = (bf16[128,1024]{1,0:T(8,128)(2,1)S(1)}, bf16[128,1024]{1,0:T(8,128)(2,1)S(1)}, u32[]{:S(2)}, u32[]{:S(2)}) collective-permute-start(bf16[128,1024]{1,0:T(8,128)(2,1)S(1)} %copy-done.7), channel_id=1, source_target_pairs={{0,2},{1,3},{2,0},{3,1},{4,6},{5,7},{6,4},{7,5},{8,10},{9,11},{10,... | collective-permute-start | bytes 786440 | tf_op jit(solution)/shard_map/ppermute | solution.py:381
  80.6 27.4 %collective-permute-start.19 = (bf16[128,1024]{1,0:T(8,128)(2,1)S(1)}, bf16[128,1024]{1,0:T(8,128)(2,1)S(1)}, u32[]{:S(2)}, u32[]{:S(2)}) collective-permute-start(bf16[128,1024]{1,0:T(8,128)(2,1)S(1)} %copy-done.6), channel_id=1, source_target_pairs={{0,2},{1,3},{2,0},{3,1},{4,6},{5,7},{6,4},{7,5},{8,10},{9,11},{10,... | collective-permute-start | bytes 786440 | tf_op jit(solution)/shard_map/ppermute | solution.py:381
  80.7 27.3 %collective-permute-start.20 = (bf16[128,1024]{1,0:T(8,128)(2,1)S(1)}, bf16[128,1024]{1,0:T(8,128)(2,1)S(1)}, u32[]{:S(2)}, u32[]{:S(2)}) collective-permute-start(bf16[128,1024]{1,0:T(8,128)(2,1)S(1)} %partial_product.10), channel_id=1, source_target_pairs={{0,1},{1,0},{2,3},{3,2},{4,5},{5,4},{6,7},{7,6},{8,9},{9,8},{10,11... | collective-permute-start | bytes 786440 | tf_op jit(solution)/shard_map/ppermute | solution.py:381
  84.0 13.5 %copy-start.5 = (bf16[128,1024]{1,0:T(8,128)(2,1)S(1)}, bf16[128,1024]{1,0:T(8,128)(2,1)}, u32[]{:S(2)}) copy-start(bf16[128,1024]{1,0:T(8,128)(2,1)} %get-tuple-element.70.x_ref.refs_0_) | copy-start | bytes 786436
  97.4 16.2 %collective-permute-start.17 = (bf16[128,1024]{1,0:T(8,128)(2,1)S(1)}, bf16[128,1024]{1,0:T(8,128)(2,1)S(1)}, u32[]{:S(2)}, u32[]{:S(2)}) collective-permute-start(bf16[128,1024]{1,0:T(8,128)(2,1)S(1)} %copy-done.5), channel_id=1, source_target_pairs={{0,2},{1,3},{2,0},{3,1},{4,6},{5,7},{6,4},{7,5},{8,10},{9,11},{10,... | collective-permute-start | bytes 786440 | tf_op jit(solution)/shard_map/ppermute | solution.py:381
  97.5 19.0 %collective-permute-start.18 = (bf16[128,1024]{1,0:T(8,128)(2,1)S(1)}, bf16[128,1024]{1,0:T(8,128)(2,1)S(1)}, u32[]{:S(2)}, u32[]{:S(2)}) collective-permute-start(bf16[128,1024]{1,0:T(8,128)(2,1)S(1)} %partial_product.11), channel_id=1, source_target_pairs={{0,1},{1,0},{2,3},{3,2},{4,5},{5,4},{6,7},{7,6},{8,9},{9,8},{10,11... | collective-permute-start | bytes 786440 | tf_op jit(solution)/shard_map/ppermute | solution.py:381
  100.5 8.4 %copy-start.4 = (bf16[128,1024]{1,0:T(8,128)(2,1)S(1)}, bf16[128,1024]{1,0:T(8,128)(2,1)}, u32[]{:S(2)}) copy-start(bf16[128,1024]{1,0:T(8,128)(2,1)} %get-tuple-element.81.x_ref.refs_0_) | copy-start | bytes 786436
  108.8 18.9 %collective-permute-start.24 = (bf16[128,1024]{1,0:T(8,128)(2,1)S(1)}, bf16[128,1024]{1,0:T(8,128)(2,1)S(1)}, u32[]{:S(2)}, u32[]{:S(2)}) collective-permute-start(bf16[128,1024]{1,0:T(8,128)(2,1)S(1)} %partial_product.12), channel_id=1, source_target_pairs={{0,1},{1,0},{2,3},{3,2},{4,5},{5,4},{6,7},{7,6},{8,9},{9,8},{10,11... | collective-permute-start | bytes 786440 | tf_op jit(solution)/shard_map/ppermute | solution.py:381
  108.9 18.8 %collective-permute-start.23 = (bf16[128,1024]{1,0:T(8,128)(2,1)S(1)}, bf16[128,1024]{1,0:T(8,128)(2,1)S(1)}, u32[]{:S(2)}, u32[]{:S(2)}) collective-permute-start(bf16[128,1024]{1,0:T(8,128)(2,1)S(1)} %copy-done.4), channel_id=1, source_target_pairs={{0,2},{1,3},{2,0},{3,1},{4,6},{5,7},{6,4},{7,5},{8,10},{9,11},{10,... | collective-permute-start | bytes 786440 | tf_op jit(solution)/shard_map/ppermute | solution.py:381
  117.3 17.4 %collective-permute-start.22 = (bf16[128,1024]{1,0:T(8,128)(2,1)S(1)}, bf16[128,1024]{1,0:T(8,128)(2,1)S(1)}, u32[]{:S(2)}, u32[]{:S(2)}) collective-permute-start(bf16[128,1024]{1,0:T(8,128)(2,1)S(1)} %partial_product.13), channel_id=1, source_target_pairs={{0,1},{1,0},{2,3},{3,2},{4,5},{5,4},{6,7},{7,6},{8,9},{9,8},{10,11... | collective-permute-start | bytes 786440 | tf_op jit(solution)/shard_map/ppermute | solution.py:381
  118.9 0.9 copy-start.3
  119.8 16.0 %collective-permute-start.21 = (bf16[128,1024]{1,0:T(8,128)(2,1)S(1)}, bf16[128,1024]{1,0:T(8,128)(2,1)S(1)}, u32[]{:S(2)}, u32[]{:S(2)}) collective-permute-start(bf16[128,1024]{1,0:T(8,128)(2,1)S(1)} %copy-done.3), channel_id=1, source_target_pairs={{0,2},{1,3},{2,0},{3,1},{4,6},{5,7},{6,4},{7,5},{8,10},{9,11},{10,... | collective-permute-start | bytes 786440 | tf_op jit(solution)/shard_map/ppermute | solution.py:381
  128.4 13.0 %collective-permute-start.26 = (bf16[128,1024]{1,0:T(8,128)(2,1)S(1)}, bf16[128,1024]{1,0:T(8,128)(2,1)S(1)}, u32[]{:S(2)}, u32[]{:S(2)}) collective-permute-start(bf16[128,1024]{1,0:T(8,128)(2,1)S(1)} %partial_product.14), channel_id=1, source_target_pairs={{0,1},{1,0},{2,3},{3,2},{4,5},{5,4},{6,7},{7,6},{8,9},{9,8},{10,11... | collective-permute-start | bytes 786440 | tf_op jit(solution)/shard_map/ppermute | solution.py:381
  136.6 10.5 %collective-permute-start.25 = (bf16[128,1024]{1,0:T(8,128)(2,1)S(1)}, bf16[128,1024]{1,0:T(8,128)(2,1)S(1)}, u32[]{:S(2)}, u32[]{:S(2)}) collective-permute-start(bf16[128,1024]{1,0:T(8,128)(2,1)S(1)} %partial_product.15), channel_id=1, source_target_pairs={{0,1},{1,0},{2,3},{3,2},{4,5},{5,4},{6,7},{7,6},{8,9},{9,8},{10,11... | collective-permute-start | bytes 786440 | tf_op jit(solution)/shard_map/ppermute | solution.py:381

commit v2 on v1

--- a/solution.py
+++ b/solution.py
@@ -137,7 +137,7 @@
             num_scalar_prefetch=3, grid=(steps,), in_specs=in_specs, out_specs=out_specs
         ),
         out_shape=out_shape,
-        compiler_params=pltpu.CompilerParams(vmem_limit_bytes=53 << 20),
+        compiler_params=LARGE,
         cost_estimate=FREE,
         name="key_side",
     )(core, place, turn, *operands)
@@ -201,7 +201,7 @@
             jax.ShapeDtypeStruct((heads, rows, 2 * count), BF16),
             jax.ShapeDtypeStruct((rows, heads * width), BF16),
         ],
-        compiler_params=MIDDLE,
+        compiler_params=LARGE,
         cost_estimate=FREE,
         name="query_side",
     )(query_rows, value_rows, frequencies, key_feat)

time: 148 us -> 149 us (level)
  waiting for transfers between devices: 67.5 us -> 70.6 us
  starting transfers between devices: 31.7 us -> 28.7 us
    ppermute x24, waiting for transfers between devices: 67.4 us -> 70.5 us  [swap(): lax.ppermute(value, axis, [(i, i ^ distance) for i in range(lax.axis_size...]
    ppermute x24, starting transfers between devices: 23.5 us -> 20.4 us  [swap(): lax.ppermute(value, axis, [(i, i ^ distance) for i in range(lax.axis_size...]
    unnamed x28 -> x26, local copies, waits for them, and re-layouts: 4.57 us -> 3.62 us
  transfers between devices with their start and end apart: 27 -> 27, of which waited for: 17 -> 16; matrix products, arithmetic and copies ran while one was open for 0% -> 1% of each run, Pallas kernels for 23% -> 23%
where the time goes in v2:
time: 149 us; the launch traced here: 148 us
  waiting for transfers between devices  70.6 us (47%)
  Pallas kernels  43.4 us (29%)
  starting transfers between devices  28.7 us (19%)
  local copies, waits for them, and re-layouts  3.69 us (2%)
    ppermute x24, waiting for transfers between devices, swap(): lax.ppermute(value, axis, [(i, i ^ distance) for i in range(lax.axis_size...  70.5 us
    ppermute x24, starting transfers between devices, swap(): lax.ppermute(value, axis, [(i, i ^ distance) for i in range(lax.axis_size...  20.4 us
    pallas_call x1, Pallas kernels, query_side(): pl.pallas_call(query_kernel, grid=(heads // group,), in_specs=[pl.BlockSp...  9.8 us
    ppermute x3, starting transfers between devices, earlier_states(): theirs = lax.ppermute(total, 'ctx', pairs)  8.25 us
    pallas_call x1, Pallas kernels, key_side(): pl.pallas_call(functools.partial(key_kernel, weight is not None), grid_sp...  8.16 us
    pallas_call x2, Pallas kernels, finish(): pl.pallas_call(functools.partial(finish_kernel, group, span, cuts), grid_...  7.66 us
    pallas_call x8, Pallas kernels, join(): pl.pallas_call(join_kernel, grid=(size // step,), in_specs=[spec, spec] +...  6.05 us
    pallas_call x8, Pallas kernels, project(): pl.pallas_call(functools.partial(project_kernel, sources), grid_spec=pltp...  5.87 us
  transfers between devices with their start and end apart: 27, of which 16 were waited for; matrix products, arithmetic and copies ran while one was open for 1% of the time, Pallas kernels for 23%

profile of v2, /device:TPU:0, one launch (start us, length us, event | category | flops | bytes accessed | tf_op | source)
XLA Modules:
  0.0 148.0 jit_solution(5785929304805957696)
XLA Ops:
  0.0 8.2 %key_side.1 = (bf16[8,256,1024]{2,1,0:T(8,128)(2,1)}, bf16[4,256,128]{2,1,0:T(8,128)(2,1)}, bf16[4,256,128]{2,1,0:T(8,128)(2,1)}, f32[8,1,256,128]{3,2,1,0:T(8,128)}, bf16[512,1024]{1,0:T(8,128)(2,1)}) custom-call(s32[1]{0:T(128)} %bitcast.1.core_ref, s32[1]{0:T(128)} %bitcast.place_ref, s32[1]{0:T(128)} %bitcast.2.turn_ref, bf16[1024,1024]{1,0:T(8,128)(2,1)} %key_ref.1, ...), custom_call_target="tpu_custom_call" | custom-call | tf_op jit(solution)/shard_map/key_side/pallas_call | solution.py:134
  8.7 2.6 %collective-permute-start.1 = (bf16[512,1024]{1,0:T(8,128)(2,1)}, bf16[512,1024]{1,0:T(8,128)(2,1)S(1)}, u32[]{:S(2)}, u32[]{:S(2)}) collective-permute-start(bf16[512,1024]{1,0:T(8,128)(2,1)} %get-tuple-element.50), channel_id=1, source_target_pairs={{0,1},{1,0},{2,3},{3,2},{4,5},{5,4},{6,7},{7,6},{8,9},{9,8},{10,11... | collective-permute-start | bytes 3145736 | tf_op jit(solution)/shard_map/ppermute | solution.py:381
  11.3 1.0 fusion.2
  12.3 3.5 %collective-permute-start.2 = (bf16[4,256,128]{2,1,0:T(8,128)(2,1)S(1)}, bf16[4,256,128]{2,1,0:T(8,128)(2,1)S(1)}, u32[]{:S(2)}, u32[]{:S(2)}) collective-permute-start(bf16[4,256,128]{2,1,0:T(8,128)(2,1)S(1)} %fusion.2), channel_id=1, source_target_pairs={{0,8},{4,12},{16,24},{20,28},{1,9},{5,13},{17,25},{21,29},{2,10},{... | collective-permute-start | bytes 786440 | tf_op jit(solution)/shard_map/ppermute | solution.py:399
  15.8 3.4 %collective-permute-start.3 = (bf16[4,256,128]{2,1,0:T(8,128)(2,1)S(1)}, bf16[4,256,128]{2,1,0:T(8,128)(2,1)S(1)}, u32[]{:S(2)}, u32[]{:S(2)}) collective-permute-start(bf16[4,256,128]{2,1,0:T(8,128)(2,1)S(1)} %fusion.2), channel_id=1, source_target_pairs={{0,16},{4,20},{8,24},{12,28},{1,17},{5,21},{9,25},{13,29},{2,18},{... | collective-permute-start | bytes 786440 | tf_op jit(solution)/shard_map/ppermute | solution.py:399
  19.3 1.3 collective-permute-start.4
  20.6 9.8 %query_side.1 = (bf16[8,1024,256]{2,1,0:T(8,128)(2,1)}, bf16[1024,1024]{1,0:T(8,128)(2,1)}) custom-call(bf16[1024,1024]{1,0:T(8,128)(2,1)} %query_ref.1, bf16[1024,1024]{1,0:T(8,128)(2,1)} %value_ref.3, bf16[8,128,128]{2,1,0:T(8,128)(2,1)} %freq_ref.2, bf16[8,256,1024]{2,1,0:T(8,128)(2,1)} %get-tuple-element.48.key_feat_ref), custom_call_target="tpu_custom_call" | custom-call | tf_op jit(solution)/shard_map/query_side/pallas_call | solution.py:187
  30.9 1.5 %collective-permute-done.5.theirs_ref = bf16[4,256,128]{2,1,0:T(8,128)(2,1)S(1)} collective-permute-done((bf16[4,256,128]{2,1,0:T(8,128)(2,1)S(1)}, bf16[4,256,128]{2,1,0:T(8,128)(2,1)S(1)}, u32[]{:S(2)}, u32[]{:S(2)}) %collective-permute-start.5) | collective-permute-done | bytes 262176 | tf_op jit(solution)/shard_map/ppermute | solution.py:381
  32.4 1.8 %finish.2.x_ref.refs_0_ = bf16[128,1024]{1,0:T(8,128)(2,1)S(1)} custom-call(s32[1]{0:T(128)} %bitcast.1.core_ref, bf16[8,1024,256]{2,1,0:T(8,128)(2,1)} %get-tuple-element.56.feat_ref, bf16[1024,1024]{1,0:T(8,128)(2,1)} %get-tuple-element.51.local_ref, bf16[4,256,128]{2,1,0:T(8,128)(2,1)S(1)} %collective-permute-done.5.theirs_ref, ...), custom_call_target="tpu_custom_call" | custom-call | tf_op jit(solution)/shard_map/finish/pallas_call | solution.py:262
  34.2 2.7 %collective-permute-start.7 = (bf16[128,1024]{1,0:T(8,128)(2,1)S(1)}, bf16[128,1024]{1,0:T(8,128)(2,1)S(1)}, u32[]{:S(2)}, u32[]{:S(2)}) collective-permute-start(bf16[128,1024]{1,0:T(8,128)(2,1)S(1)} %finish.2.x_ref.refs_0_), channel_id=1, source_target_pairs={{0,2},{1,3},{2,0},{3,1},{4,6},{5,7},{6,4},{7,5},{8,10},{9,11},{10,... | collective-permute-start | bytes 786440 | tf_op jit(solution)/shard_map/ppermute | solution.py:381
  37.0 2.5 %collective-permute-start.9 = (bf16[256,1024]{1,0:T(8,128)(2,1)S(1)}, bf16[256,1024]{1,0:T(8,128)(2,1)S(1)}, u32[]{:S(2)}, u32[]{:S(2)}) collective-permute-start(bf16[256,1024]{1,0:T(8,128)(2,1)S(1)} %get-tuple-element.85), channel_id=1, source_target_pairs={{0,16},{4,20},{8,24},{12,28},{16,0},{20,4},{24,8},{28,12},{1,17},{... | collective-permute-start | bytes 1572872 | tf_op jit(solution)/shard_map/ppermute | solution.py:381
  39.5 5.8 %finish.3 = (bf16[128,1024]{1,0:T(8,128)(2,1)}, bf16[128,1024]{1,0:T(8,128)(2,1)}, bf16[128,1024]{1,0:T(8,128)(2,1)}, bf16[128,1024]{1,0:T(8,128)(2,1)}, bf16[12...) custom-call(s32[1]{0:T(128)} %bitcast.1.core_ref, ...), custom_call_target="tpu_custom_call" | custom-call | tf_op jit(solution)/shard_map/finish/pallas_call | solution.py:262
  45.3 3.8 %collective-permute-done.7.y_ref.refs_1_ = bf16[128,1024]{1,0:T(8,128)(2,1)S(1)} collective-permute-done((bf16[128,1024]{1,0:T(8,128)(2,1)S(1)}, bf16[128,1024]{1,0:T(8,128)(2,1)S(1)}, u32[]{:S(2)}, u32[]{:S(2)}) %collective-permute-start.7) | collective-permute-done | bytes 262176 | tf_op jit(solution)/shard_map/ppermute | solution.py:381
  49.2 2.3 %collective-permute-done.9.refs_2_ = bf16[256,1024]{1,0:T(8,128)(2,1)S(1)} collective-permute-done((bf16[256,1024]{1,0:T(8,128)(2,1)S(1)}, bf16[256,1024]{1,0:T(8,128)(2,1)S(1)}, u32[]{:S(2)}, u32[]{:S(2)}) %collective-permute-start.9) | collective-permute-done | bytes 524320 | tf_op jit(solution)/shard_map/ppermute | solution.py:381
  51.4 1.5 collective-permute-done.8.refs_1_
  53.4 1.5 collective-permute-done.11.refs_4_
  55.6 1.6 %collective-permute-start.13 = (bf16[128,1024]{1,0:T(8,128)(2,1)S(1)}, bf16[128,1024]{1,0:T(8,128)(2,1)S(1)}, u32[]{:S(2)}, u32[]{:S(2)}) collective-permute-start(bf16[128,1024]{1,0:T(8,128)(2,1)S(1)} %partial_product.8), channel_id=1, source_target_pairs={{0,1},{1,0},{2,3},{3,2},{4,5},{5,4},{6,7},{7,6},{8,9},{9,8},{10,11... | collective-permute-start | bytes 786440 | tf_op jit(solution)/shard_map/ppermute | solution.py:381
  57.2 1.0 collective-permute-start.16
  58.2 3.4 %copy-done = bf16[4096,1024]{1,0:T(8,128)(2,1)S(1)} copy-done((bf16[4096,1024]{1,0:T(8,128)(2,1)S(1)}, bf16[4096,1024]{1,0:T(8,128)(2,1)}, u32[]{:S(2)}) %copy-start) | copy-done | bytes 8388632
  61.6 0.7 project.8.a_ref
  62.4 6.5 %collective-permute-done.6.y_ref.refs_1_ = bf16[128,1024]{1,0:T(8,128)(2,1)S(1)} collective-permute-done((bf16[128,1024]{1,0:T(8,128)(2,1)}, bf16[128,1024]{1,0:T(8,128)(2,1)S(1)}, u32[]{:S(2)}, u32[]{:S(2)}) %collective-permute-start.6) | collective-permute-done | bytes 262176 | tf_op jit(solution)/shard_map/ppermute | solution.py:381
  68.8 0.7 partial_product.9
  69.7 1.8 %collective-permute-start.14 = (bf16[128,1024]{1,0:T(8,128)(2,1)S(1)}, bf16[128,1024]{1,0:T(8,128)(2,1)S(1)}, u32[]{:S(2)}, u32[]{:S(2)}) collective-permute-start(bf16[128,1024]{1,0:T(8,128)(2,1)S(1)} %copy-done.7), channel_id=1, source_target_pairs={{0,2},{1,3},{2,0},{3,1},{4,6},{5,7},{6,4},{7,5},{8,10},{9,11},{10,... | collective-permute-start | bytes 786440 | tf_op jit(solution)/shard_map/ppermute | solution.py:381
  71.5 8.6 %collective-permute-done.16.y_ref.refs_1_ = bf16[128,1024]{1,0:T(8,128)(2,1)S(1)} collective-permute-done((bf16[128,1024]{1,0:T(8,128)(2,1)S(1)}, bf16[128,1024]{1,0:T(8,128)(2,1)S(1)}, u32[]{:S(2)}, u32[]{:S(2)}) %collective-permute-start.16) | collective-permute-done | bytes 262176 | tf_op jit(solution)/shard_map/ppermute | solution.py:381
  80.9 1.8 %collective-permute-start.20 = (bf16[128,1024]{1,0:T(8,128)(2,1)S(1)}, bf16[128,1024]{1,0:T(8,128)(2,1)S(1)}, u32[]{:S(2)}, u32[]{:S(2)}) collective-permute-start(bf16[128,1024]{1,0:T(8,128)(2,1)S(1)} %partial_product.10), channel_id=1, source_target_pairs={{0,1},{1,0},{2,3},{3,2},{4,5},{5,4},{6,7},{7,6},{8,9},{9,8},{10,11... | collective-permute-start | bytes 786440 | tf_op jit(solution)/shard_map/ppermute | solution.py:381
  83.5 13.5 %collective-permute-done.14.y_ref.refs_1_ = bf16[128,1024]{1,0:T(8,128)(2,1)S(1)} collective-permute-done((bf16[128,1024]{1,0:T(8,128)(2,1)S(1)}, bf16[128,1024]{1,0:T(8,128)(2,1)S(1)}, u32[]{:S(2)}, u32[]{:S(2)}) %collective-permute-start.14) | collective-permute-done | bytes 262176 | tf_op jit(solution)/shard_map/ppermute | solution.py:381
  97.8 1.4 collective-permute-start.18
  99.9 8.3 %collective-permute-done.19.y_ref.refs_1_ = bf16[128,1024]{1,0:T(8,128)(2,1)S(1)} collective-permute-done((bf16[128,1024]{1,0:T(8,128)(2,1)S(1)}, bf16[128,1024]{1,0:T(8,128)(2,1)S(1)}, u32[]{:S(2)}, u32[]{:S(2)}) %collective-permute-start.19) | collective-permute-done | bytes 262176 | tf_op jit(solution)/shard_map/ppermute | solution.py:381
  108.3 0.7 partial_product.12
  109.1 1.4 collective-permute-start.23
  111.3 2.6 %collective-permute-done.17.y_ref.refs_1_ = bf16[128,1024]{1,0:T(8,128)(2,1)S(1)} collective-permute-done((bf16[128,1024]{1,0:T(8,128)(2,1)S(1)}, bf16[128,1024]{1,0:T(8,128)(2,1)S(1)}, u32[]{:S(2)}, u32[]{:S(2)}) %collective-permute-start.17) | collective-permute-done | bytes 262176 | tf_op jit(solution)/shard_map/ppermute | solution.py:381
  113.9 2.1 %collective-permute-done.18.b_ref = bf16[128,1024]{1,0:T(8,128)(2,1)S(1)} collective-permute-done((bf16[128,1024]{1,0:T(8,128)(2,1)S(1)}, bf16[128,1024]{1,0:T(8,128)(2,1)S(1)}, u32[]{:S(2)}, u32[]{:S(2)}) %collective-permute-start.18) | collective-permute-done | bytes 262176 | tf_op jit(solution)/shard_map/ppermute | solution.py:381
  116.8 0.8 join.8.refs_0_
  117.5 0.7 join.9.refs_0_
  118.3 0.8 join.10.refs_0_
  119.2 2.1 %collective-permute-start.21 = (bf16[128,1024]{1,0:T(8,128)(2,1)S(1)}, bf16[128,1024]{1,0:T(8,128)(2,1)S(1)}, u32[]{:S(2)}, u32[]{:S(2)}) collective-permute-start(bf16[128,1024]{1,0:T(8,128)(2,1)S(1)} %copy-done.3), channel_id=1, source_target_pairs={{0,2},{1,3},{2,0},{3,1},{4,6},{5,7},{6,4},{7,5},{8,10},{9,11},{10,... | collective-permute-start | bytes 786440 | tf_op jit(solution)/shard_map/ppermute | solution.py:381
  122.1 5.1 %collective-permute-done.24.b_ref = bf16[128,1024]{1,0:T(8,128)(2,1)S(1)} collective-permute-done((bf16[128,1024]{1,0:T(8,128)(2,1)S(1)}, bf16[128,1024]{1,0:T(8,128)(2,1)S(1)}, u32[]{:S(2)}, u32[]{:S(2)}) %collective-permute-start.24) | collective-permute-done | bytes 262176 | tf_op jit(solution)/shard_map/ppermute | solution.py:381
  128.0 0.7 project.14.a_ref
  128.7 7.4 %collective-permute-done.22.b_ref = bf16[128,1024]{1,0:T(8,128)(2,1)S(1)} collective-permute-done((bf16[128,1024]{1,0:T(8,128)(2,1)S(1)}, bf16[128,1024]{1,0:T(8,128)(2,1)S(1)}, u32[]{:S(2)}, u32[]{:S(2)}) %collective-permute-start.22) | collective-permute-done | bytes 262176 | tf_op jit(solution)/shard_map/ppermute | solution.py:381
  136.9 0.7 project.15.a_ref
  137.6 0.8 join.11.refs_0_
  138.4 0.7 join.12.refs_0_
  139.1 0.8 project.12.a_ref
  139.9 0.8 join.13.refs_0_
  140.7 1.0 collective-permute-done.26.b_ref
  141.7 0.7 join.14.refs_0_
  142.4 4.9 %collective-permute-done.25.b_ref = bf16[128,1024]{1,0:T(8,128)(2,1)S(1)} collective-permute-done((bf16[128,1024]{1,0:T(8,128)(2,1)S(1)}, bf16[128,1024]{1,0:T(8,128)(2,1)S(1)}, u32[]{:S(2)}, u32[]{:S(2)}) %collective-permute-start.25) | collective-permute-done | bytes 262176 | tf_op jit(solution)/shard_map/ppermute | solution.py:381
  147.3 0.8 join.15
  (63 shorter events, 9.5 us)
Async XLA Ops:
  8.2 3.1 %collective-permute-start = (bf16[4,256,128]{2,1,0:T(8,128)(2,1)}, bf16[4,256,128]{2,1,0:T(8,128)(2,1)S(1)}, u32[]{:S(2)}, u32[]{:S(2)}) collective-permute-start(bf16[4,256,128]{2,1,0:T(8,128)(2,1)} %get-tuple-element.46), channel_id=1, source_target_pairs={{0,4},{4,0},{8,12},{12,8},{16,20},{20,16},{24,28},{28,24},{1,5},{5... | collective-permute-start | bytes 786440 | tf_op jit(solution)/shard_map/ppermute | solution.py:381
  8.7 28.2 %collective-permute-start.1 = (bf16[512,1024]{1,0:T(8,128)(2,1)}, bf16[512,1024]{1,0:T(8,128)(2,1)S(1)}, u32[]{:S(2)}, u32[]{:S(2)}) collective-permute-start(bf16[512,1024]{1,0:T(8,128)(2,1)} %get-tuple-element.50), channel_id=1, source_target_pairs={{0,1},{1,0},{2,3},{3,2},{4,5},{5,4},{6,7},{7,6},{8,9},{9,8},{10,11... | collective-permute-start | bytes 3145736 | tf_op jit(solution)/shard_map/ppermute | solution.py:381
  12.3 18.1 %collective-permute-start.2 = (bf16[4,256,128]{2,1,0:T(8,128)(2,1)S(1)}, bf16[4,256,128]{2,1,0:T(8,128)(2,1)S(1)}, u32[]{:S(2)}, u32[]{:S(2)}) collective-permute-start(bf16[4,256,128]{2,1,0:T(8,128)(2,1)S(1)} %fusion.2), channel_id=1, source_target_pairs={{0,8},{4,12},{16,24},{20,28},{1,9},{5,13},{17,25},{21,29},{2,10},{... | collective-permute-start | bytes 786440 | tf_op jit(solution)/shard_map/ppermute | solution.py:399
  15.8 14.6 %collective-permute-start.3 = (bf16[4,256,128]{2,1,0:T(8,128)(2,1)S(1)}, bf16[4,256,128]{2,1,0:T(8,128)(2,1)S(1)}, u32[]{:S(2)}, u32[]{:S(2)}) collective-permute-start(bf16[4,256,128]{2,1,0:T(8,128)(2,1)S(1)} %fusion.2), channel_id=1, source_target_pairs={{0,16},{4,20},{8,24},{12,28},{1,17},{5,21},{9,25},{13,29},{2,18},{... | collective-permute-start | bytes 786440 | tf_op jit(solution)/shard_map/ppermute | solution.py:399
  19.3 11.2 %collective-permute-start.4 = (bf16[4,256,128]{2,1,0:T(8,128)(2,1)S(1)}, bf16[4,256,128]{2,1,0:T(8,128)(2,1)S(1)}, u32[]{:S(2)}, u32[]{:S(2)}) collective-permute-start(bf16[4,256,128]{2,1,0:T(8,128)(2,1)S(1)} %fusion.2), channel_id=1, source_target_pairs={{0,24},{4,28},{8,16},{12,20},{1,25},{5,29},{9,17},{13,21},{2,26},{... | collective-permute-start | bytes 786440 | tf_op jit(solution)/shard_map/ppermute | solution.py:399
  20.6 9.8 %copy-start.12 = (bf16[4,256,128]{2,1,0:T(8,128)(2,1)S(1)}, bf16[4,256,128]{2,1,0:T(8,128)(2,1)}, u32[]{:S(2)}) copy-start(bf16[4,256,128]{2,1,0:T(8,128)(2,1)} %get-tuple-element.45) | copy-start | bytes 786436
  20.6 11.7 %copy-start.11 = (bf16[1024]{0:T(1024)(128)(2,1)S(1)}, bf16[1024]{0:T(1024)(128)(2,1)}, u32[]{:S(2)}) copy-start(bf16[1024]{0:T(1024)(128)(2,1)} %param.10) | copy-start | bytes 6148
  30.8 3.4 %copy-start.2 = (bf16[4,256,128]{2,1,0:T(8,128)(2,1)}, bf16[4,256,128]{2,1,0:T(8,128)(2,1)S(1)}, u32[]{:S(2)}) copy-start(bf16[4,256,128]{2,1,0:T(8,128)(2,1)S(1)} %get-tuple-element.87.mine_ref) | copy-start | bytes 786436
  30.8 1.6 %collective-permute-start.5 = (bf16[4,256,128]{2,1,0:T(8,128)(2,1)S(1)}, bf16[4,256,128]{2,1,0:T(8,128)(2,1)S(1)}, u32[]{:S(2)}, u32[]{:S(2)}) collective-permute-start(bf16[4,256,128]{2,1,0:T(8,128)(2,1)S(1)} %get-tuple-element.88), channel_id=1, source_target_pairs={{0,4},{4,0},{8,12},{12,8},{16,20},{20,16},{24,28},{28,24},{1,5},{5... | collective-permute-start | bytes 786440 | tf_op jit(solution)/shard_map/ppermute | solution.py:381
  32.4 1.8 %copy-start.10 = (bf16[4,256,128]{2,1,0:T(8,128)(2,1)}, bf16[4,256,128]{2,1,0:T(8,128)(2,1)S(1)}, u32[]{:S(2)}) copy-start(bf16[4,256,128]{2,1,0:T(8,128)(2,1)S(1)} %collective-permute-done.5.theirs_ref) | copy-start | bytes 786436
  34.2 14.9 %collective-permute-start.7 = (bf16[128,1024]{1,0:T(8,128)(2,1)S(1)}, bf16[128,1024]{1,0:T(8,128)(2,1)S(1)}, u32[]{:S(2)}, u32[]{:S(2)}) collective-permute-start(bf16[128,1024]{1,0:T(8,128)(2,1)S(1)} %finish.2.x_ref.refs_0_), channel_id=1, source_target_pairs={{0,2},{1,3},{2,0},{3,1},{4,6},{5,7},{6,4},{7,5},{8,10},{9,11},{10,... | collective-permute-start | bytes 786440 | tf_op jit(solution)/shard_map/ppermute | solution.py:381
  37.0 14.5 %collective-permute-start.9 = (bf16[256,1024]{1,0:T(8,128)(2,1)S(1)}, bf16[256,1024]{1,0:T(8,128)(2,1)S(1)}, u32[]{:S(2)}, u32[]{:S(2)}) collective-permute-start(bf16[256,1024]{1,0:T(8,128)(2,1)S(1)} %get-tuple-element.85), channel_id=1, source_target_pairs={{0,16},{4,20},{8,24},{12,28},{16,0},{20,4},{24,8},{28,12},{1,17},{... | collective-permute-start | bytes 1572872 | tf_op jit(solution)/shard_map/ppermute | solution.py:381
  39.5 13.4 %collective-permute-start.8 = (bf16[256,1024]{1,0:T(8,128)(2,1)S(1)}, bf16[256,1024]{1,0:T(8,128)(2,1)S(1)}, u32[]{:S(2)}, u32[]{:S(2)}) collective-permute-start(bf16[256,1024]{1,0:T(8,128)(2,1)S(1)} %get-tuple-element.86), channel_id=1, source_target_pairs={{0,8},{4,12},{8,0},{12,4},{16,24},{20,28},{24,16},{28,20},{1,9},{5... | collective-permute-start | bytes 1572872 | tf_op jit(solution)/shard_map/ppermute | solution.py:381
  49.2 5.7 %collective-permute-start.10 = (bf16[512,1024]{1,0:T(8,128)(2,1)S(1)}, bf16[512,1024]{1,0:T(8,128)(2,1)S(1)}, u32[]{:S(2)}, u32[]{:S(2)}) collective-permute-start(bf16[512,1024]{1,0:T(8,128)(2,1)S(1)} %collective-permute-done.1.refs_0_), channel_id=1, source_target_pairs={{0,4},{4,0},{8,12},{12,8},{16,20},{20,16},{24,28},{28,24},{1,5},{5... | collective-permute-start | bytes 3145736 | tf_op jit(solution)/shard_map/ppermute | solution.py:381
  51.4 1.9 %collective-permute-start.12 = (bf16[256,1024]{1,0:T(8,128)(2,1)S(1)}, bf16[256,1024]{1,0:T(8,128)(2,1)S(1)}, u32[]{:S(2)}, u32[]{:S(2)}) collective-permute-start(bf16[256,1024]{1,0:T(8,128)(2,1)S(1)} %collective-permute-done.9.refs_2_), channel_id=1, source_target_pairs={{0,4},{4,0},{8,12},{12,8},{16,20},{20,16},{24,28},{28,24},{1,5},{5... | collective-permute-start | bytes 1572872 | tf_op jit(solution)/shard_map/ppermute | solution.py:381
  52.9 1.9 %collective-permute-start.11 = (bf16[256,1024]{1,0:T(8,128)(2,1)S(1)}, bf16[256,1024]{1,0:T(8,128)(2,1)S(1)}, u32[]{:S(2)}, u32[]{:S(2)}) collective-permute-start(bf16[256,1024]{1,0:T(8,128)(2,1)S(1)} %collective-permute-done.8.refs_1_), channel_id=1, source_target_pairs={{0,4},{4,0},{8,12},{12,8},{16,20},{20,16},{24,28},{28,24},{1,5},{5... | collective-permute-start | bytes 1572872 | tf_op jit(solution)/shard_map/ppermute | solution.py:381
  52.9 4.3 %copy-start.8 = (bf16[128,1024]{1,0:T(8,128)(2,1)S(1)}, bf16[128,1024]{1,0:T(8,128)(2,1)}, u32[]{:S(2)}) copy-start(bf16[128,1024]{1,0:T(8,128)(2,1)} %get-tuple-element.67.x_ref.refs_0_) | copy-start | bytes 786436
  52.9 15.9 %collective-permute-start.6 = (bf16[128,1024]{1,0:T(8,128)(2,1)}, bf16[128,1024]{1,0:T(8,128)(2,1)S(1)}, u32[]{:S(2)}, u32[]{:S(2)}) collective-permute-start(bf16[128,1024]{1,0:T(8,128)(2,1)} %get-tuple-element.61.x_ref.refs_0_), channel_id=1, source_target_pairs={{0,2},{1,3},{2,0},{3,1},{4,6},{5,7},{6,4},{7,5},{8,10},{9,11},{10,... | collective-permute-start | bytes 786440 | tf_op jit(solution)/shard_map/ppermute | solution.py:381
  55.6 14.1 %collective-permute-start.13 = (bf16[128,1024]{1,0:T(8,128)(2,1)S(1)}, bf16[128,1024]{1,0:T(8,128)(2,1)S(1)}, u32[]{:S(2)}, u32[]{:S(2)}) collective-permute-start(bf16[128,1024]{1,0:T(8,128)(2,1)S(1)} %partial_product.8), channel_id=1, source_target_pairs={{0,1},{1,0},{2,3},{3,2},{4,5},{5,4},{6,7},{7,6},{8,9},{9,8},{10,11... | collective-permute-start | bytes 786440 | tf_op jit(solution)/shard_map/ppermute | solution.py:381
  57.2 22.9 %collective-permute-start.16 = (bf16[128,1024]{1,0:T(8,128)(2,1)S(1)}, bf16[128,1024]{1,0:T(8,128)(2,1)S(1)}, u32[]{:S(2)}, u32[]{:S(2)}) collective-permute-start(bf16[128,1024]{1,0:T(8,128)(2,1)S(1)} %copy-done.8), channel_id=1, source_target_pairs={{0,2},{1,3},{2,0},{3,1},{4,6},{5,7},{6,4},{7,5},{8,10},{9,11},{10,... | collective-permute-start | bytes 786440 | tf_op jit(solution)/shard_map/ppermute | solution.py:381
  58.2 3.4 %copy-start = (bf16[4096,1024]{1,0:T(8,128)(2,1)S(1)}, bf16[4096,1024]{1,0:T(8,128)(2,1)}, u32[]{:S(2)}) copy-start(bf16[4096,1024]{1,0:T(8,128)(2,1)} %refs_3_.15) | copy-start | bytes 25165828
  61.6 7.2 %copy-start.9 = (bf16[128,1024]{1,0:T(8,128)(2,1)S(1)}, bf16[128,1024]{1,0:T(8,128)(2,1)}, u32[]{:S(2)}) copy-start(bf16[128,1024]{1,0:T(8,128)(2,1)} %get-tuple-element.61.x_ref.refs_0_) | copy-start | bytes 786436
  62.4 7.3 %copy-start.7 = (bf16[128,1024]{1,0:T(8,128)(2,1)S(1)}, bf16[128,1024]{1,0:T(8,128)(2,1)}, u32[]{:S(2)}) copy-start(bf16[128,1024]{1,0:T(8,128)(2,1)} %get-tuple-element.66.x_ref.refs_0_) | copy-start | bytes 786436
  68.8 13.9 %copy-start.1 = (bf16[4096,1024]{1,0:T(8,128)(2,1)S(1)}, bf16[4096,1024]{1,0:T(8,128)(2,1)}, u32[]{:S(2)}) copy-start(bf16[4096,1024]{1,0:T(8,128)(2,1)} %refs_3_.15) | copy-start | bytes 25165828
  69.6 13.9 %collective-permute-start.15 = (bf16[128,1024]{1,0:T(8,128)(2,1)S(1)}, bf16[128,1024]{1,0:T(8,128)(2,1)S(1)}, u32[]{:S(2)}, u32[]{:S(2)}) collective-permute-start(bf16[128,1024]{1,0:T(8,128)(2,1)S(1)} %partial_product.9), channel_id=1, source_target_pairs={{0,1},{1,0},{2,3},{3,2},{4,5},{5,4},{6,7},{7,6},{8,9},{9,8},{10,11... | collective-permute-start | bytes 786440 | tf_op jit(solution)/shard_map/ppermute | solution.py:381
  69.7 11.2 %copy-start.6 = (bf16[128,1024]{1,0:T(8,128)(2,1)S(1)}, bf16[128,1024]{1,0:T(8,128)(2,1)}, u32[]{:S(2)}) copy-start(bf16[128,1024]{1,0:T(8,128)(2,1)} %get-tuple-element.72.x_ref.refs_0_) | copy-start | bytes 786436
  69.7 27.2 %collective-permute-start.14 = (bf16[128,1024]{1,0:T(8,128)(2,1)S(1)}, bf16[128,1024]{1,0:T(8,128)(2,1)S(1)}, u32[]{:S(2)}, u32[]{:S(2)}) collective-permute-start(bf16[128,1024]{1,0:T(8,128)(2,1)S(1)} %copy-done.7), channel_id=1, source_target_pairs={{0,2},{1,3},{2,0},{3,1},{4,6},{5,7},{6,4},{7,5},{8,10},{9,11},{10,... | collective-permute-start | bytes 786440 | tf_op jit(solution)/shard_map/ppermute | solution.py:381
  80.9 27.4 %collective-permute-start.19 = (bf16[128,1024]{1,0:T(8,128)(2,1)S(1)}, bf16[128,1024]{1,0:T(8,128)(2,1)S(1)}, u32[]{:S(2)}, u32[]{:S(2)}) collective-permute-start(bf16[128,1024]{1,0:T(8,128)(2,1)S(1)} %copy-done.6), channel_id=1, source_target_pairs={{0,2},{1,3},{2,0},{3,1},{4,6},{5,7},{6,4},{7,5},{8,10},{9,11},{10,... | collective-permute-start | bytes 786440 | tf_op jit(solution)/shard_map/ppermute | solution.py:381
  80.9 27.3 %collective-permute-start.20 = (bf16[128,1024]{1,0:T(8,128)(2,1)S(1)}, bf16[128,1024]{1,0:T(8,128)(2,1)S(1)}, u32[]{:S(2)}, u32[]{:S(2)}) collective-permute-start(bf16[128,1024]{1,0:T(8,128)(2,1)S(1)} %partial_product.10), channel_id=1, source_target_pairs={{0,1},{1,0},{2,3},{3,2},{4,5},{5,4},{6,7},{7,6},{8,9},{9,8},{10,11... | collective-permute-start | bytes 786440 | tf_op jit(solution)/shard_map/ppermute | solution.py:381
  83.5 14.2 %copy-start.5 = (bf16[128,1024]{1,0:T(8,128)(2,1)S(1)}, bf16[128,1024]{1,0:T(8,128)(2,1)}, u32[]{:S(2)}) copy-start(bf16[128,1024]{1,0:T(8,128)(2,1)} %get-tuple-element.70.x_ref.refs_0_) | copy-start | bytes 786436
  97.7 16.2 %collective-permute-start.17 = (bf16[128,1024]{1,0:T(8,128)(2,1)S(1)}, bf16[128,1024]{1,0:T(8,128)(2,1)S(1)}, u32[]{:S(2)}, u32[]{:S(2)}) collective-permute-start(bf16[128,1024]{1,0:T(8,128)(2,1)S(1)} %copy-done.5), channel_id=1, source_target_pairs={{0,2},{1,3},{2,0},{3,1},{4,6},{5,7},{6,4},{7,5},{8,10},{9,11},{10,... | collective-permute-start | bytes 786440 | tf_op jit(solution)/shard_map/ppermute | solution.py:381
  97.8 18.2 %collective-permute-start.18 = (bf16[128,1024]{1,0:T(8,128)(2,1)S(1)}, bf16[128,1024]{1,0:T(8,128)(2,1)S(1)}, u32[]{:S(2)}, u32[]{:S(2)}) collective-permute-start(bf16[128,1024]{1,0:T(8,128)(2,1)S(1)} %partial_product.11), channel_id=1, source_target_pairs={{0,1},{1,0},{2,3},{3,2},{4,5},{5,4},{6,7},{7,6},{8,9},{9,8},{10,11... | collective-permute-start | bytes 786440 | tf_op jit(solution)/shard_map/ppermute | solution.py:381
  99.9 9.2 %copy-start.4 = (bf16[128,1024]{1,0:T(8,128)(2,1)S(1)}, bf16[128,1024]{1,0:T(8,128)(2,1)}, u32[]{:S(2)}) copy-start(bf16[128,1024]{1,0:T(8,128)(2,1)} %get-tuple-element.81.x_ref.refs_0_) | copy-start | bytes 786436
  109.0 18.1 %collective-permute-start.24 = (bf16[128,1024]{1,0:T(8,128)(2,1)S(1)}, bf16[128,1024]{1,0:T(8,128)(2,1)S(1)}, u32[]{:S(2)}, u32[]{:S(2)}) collective-permute-start(bf16[128,1024]{1,0:T(8,128)(2,1)S(1)} %partial_product.12), channel_id=1, source_target_pairs={{0,1},{1,0},{2,3},{3,2},{4,5},{5,4},{6,7},{7,6},{8,9},{9,8},{10,11... | collective-permute-start | bytes 786440 | tf_op jit(solution)/shard_map/ppermute | solution.py:381
  109.1 18.1 %collective-permute-start.23 = (bf16[128,1024]{1,0:T(8,128)(2,1)S(1)}, bf16[128,1024]{1,0:T(8,128)(2,1)S(1)}, u32[]{:S(2)}, u32[]{:S(2)}) collective-permute-start(bf16[128,1024]{1,0:T(8,128)(2,1)S(1)} %copy-done.4), channel_id=1, source_target_pairs={{0,2},{1,3},{2,0},{3,1},{4,6},{5,7},{6,4},{7,5},{8,10},{9,11},{10,... | collective-permute-start | bytes 786440 | tf_op jit(solution)/shard_map/ppermute | solution.py:381
  116.7 19.4 %collective-permute-start.22 = (bf16[128,1024]{1,0:T(8,128)(2,1)S(1)}, bf16[128,1024]{1,0:T(8,128)(2,1)S(1)}, u32[]{:S(2)}, u32[]{:S(2)}) collective-permute-start(bf16[128,1024]{1,0:T(8,128)(2,1)S(1)} %partial_product.13), channel_id=1, source_target_pairs={{0,1},{1,0},{2,3},{3,2},{4,5},{5,4},{6,7},{7,6},{8,9},{9,8},{10,11... | collective-permute-start | bytes 786440 | tf_op jit(solution)/shard_map/ppermute | solution.py:381
  118.3 0.9 copy-start.3
  119.2 16.8 %collective-permute-start.21 = (bf16[128,1024]{1,0:T(8,128)(2,1)S(1)}, bf16[128,1024]{1,0:T(8,128)(2,1)S(1)}, u32[]{:S(2)}, u32[]{:S(2)}) collective-permute-start(bf16[128,1024]{1,0:T(8,128)(2,1)S(1)} %copy-done.3), channel_id=1, source_target_pairs={{0,2},{1,3},{2,0},{3,1},{4,6},{5,7},{6,4},{7,5},{8,10},{9,11},{10,... | collective-permute-start | bytes 786440 | tf_op jit(solution)/shard_map/ppermute | solution.py:381
  127.9 13.8 %collective-permute-start.26 = (bf16[128,1024]{1,0:T(8,128)(2,1)S(1)}, bf16[128,1024]{1,0:T(8,128)(2,1)S(1)}, u32[]{:S(2)}, u32[]{:S(2)}) collective-permute-start(bf16[128,1024]{1,0:T(8,128)(2,1)S(1)} %partial_product.14), channel_id=1, source_target_pairs={{0,1},{1,0},{2,3},{3,2},{4,5},{5,4},{6,7},{7,6},{8,9},{9,8},{10,11... | collective-permute-start | bytes 786440 | tf_op jit(solution)/shard_map/ppermute | solution.py:381
  136.8 10.5 %collective-permute-start.25 = (bf16[128,1024]{1,0:T(8,128)(2,1)S(1)}, bf16[128,1024]{1,0:T(8,128)(2,1)S(1)}, u32[]{:S(2)}, u32[]{:S(2)}) collective-permute-start(bf16[128,1024]{1,0:T(8,128)(2,1)S(1)} %partial_product.15), channel_id=1, source_target_pairs={{0,1},{1,0},{2,3},{3,2},{4,5},{5,4},{6,7},{7,6},{8,9},{9,8},{10,11... | collective-permute-start | bytes 786440 | tf_op jit(solution)/shard_map/ppermute | solution.py:381

commit v3 on v1

--- a/solution.py
+++ b/solution.py
@@ -137,7 +137,7 @@
             num_scalar_prefetch=3, grid=(steps,), in_specs=in_specs, out_specs=out_specs
         ),
         out_shape=out_shape,
-        compiler_params=pltpu.CompilerParams(vmem_limit_bytes=53 << 20),
+        compiler_params=pltpu.CompilerParams(vmem_limit_bytes=213 << 18),
         cost_estimate=FREE,
         name="key_side",
     )(core, place, turn, *operands)

time: 148 us -> 147 us (level)
    unnamed x28 -> x26, local copies, waits for them, and re-layouts: 4.57 us -> 3.62 us
  transfers between devices with their start and end apart: 27 -> 27, of which waited for: 17 -> 16; matrix products, arithmetic and copies ran while one was open for 0% -> 0% of each run, Pallas kernels for 23% -> 23%
where the time goes in v3:
time: 147 us
  waiting for transfers between devices  67.9 us (46%)
  Pallas kernels  43.3 us (29%)
  starting transfers between devices  31.4 us (21%)
  local copies, waits for them, and re-layouts  3.69 us (3%)
    ppermute x24, waiting for transfers between devices, swap(): lax.ppermute(value, axis, [(i, i ^ distance) for i in range(lax.axis_size...  67.8 us
    ppermute x24, starting transfers between devices, swap(): lax.ppermute(value, axis, [(i, i ^ distance) for i in range(lax.axis_size...  23.2 us
    pallas_call x1, Pallas kernels, query_side(): pl.pallas_call(query_kernel, grid=(heads // group,), in_specs=[pl.BlockSp...  9.73 us
    ppermute x3, starting transfers between devices, earlier_states(): theirs = lax.ppermute(total, 'ctx', pairs)  8.16 us
    pallas_call x1, Pallas kernels, key_side(): pl.pallas_call(functools.partial(key_kernel, weight is not None), grid_sp...  8.12 us
    pallas_call x2, Pallas kernels, finish(): pl.pallas_call(functools.partial(finish_kernel, group, span, cuts), grid_...  7.66 us
    pallas_call x8, Pallas kernels, join(): pl.pallas_call(join_kernel, grid=(size // step,), in_specs=[spec, spec] +...  6.05 us
    pallas_call x8, Pallas kernels, project(): pl.pallas_call(functools.partial(project_kernel, sources), grid_spec=pltp...  5.85 us
  transfers between devices with their start and end apart: 27, of which 16 were waited for; matrix products, arithmetic and copies ran while one was open for 0% of the time, Pallas kernels for 23%

profile of v3, /device:TPU:0, one launch (start us, length us, event | category | flops | bytes accessed | tf_op | source)
XLA Modules:
  0.0 147.0 jit_solution(7469977950168585898)
XLA Ops:
  0.0 8.1 %key_side.1 = (bf16[8,256,1024]{2,1,0:T(8,128)(2,1)}, bf16[4,256,128]{2,1,0:T(8,128)(2,1)S(1)}, bf16[4,256,128]{2,1,0:T(8,128)(2,1)S(1)}, f32[8,1,256,128]{3,2,1,0:T(8,128)}, bf16[512,1024]{1,0:T(8,128)(2,1)}) custom-call(s32[1]{0:T(128)} %bitcast.1.core_ref, s32[1]{0:T(128)} %bitcast.place_ref, s32[1]{0:T(128)} %bitcast.2.turn_ref, ...), custom_call_target="tpu_custom_call" | custom-call | tf_op jit(solution)/shard_map/key_side/pallas_call | solution.py:134
  8.6 2.6 %collective-permute-start.1 = (bf16[512,1024]{1,0:T(8,128)(2,1)}, bf16[512,1024]{1,0:T(8,128)(2,1)S(1)}, u32[]{:S(2)}, u32[]{:S(2)}) collective-permute-start(bf16[512,1024]{1,0:T(8,128)(2,1)} %get-tuple-element.50), channel_id=1, source_target_pairs={{0,1},{1,0},{2,3},{3,2},{4,5},{5,4},{6,7},{7,6},{8,9},{9,8},{10,11... | collective-permute-start | bytes 3145736 | tf_op jit(solution)/shard_map/ppermute | solution.py:381
  11.3 3.4 %collective-permute-start.2 = (bf16[4,256,128]{2,1,0:T(8,128)(2,1)S(1)}, bf16[4,256,128]{2,1,0:T(8,128)(2,1)S(1)}, u32[]{:S(2)}, u32[]{:S(2)}) collective-permute-start(bf16[4,256,128]{2,1,0:T(8,128)(2,1)S(1)} %fusion.2), channel_id=1, source_target_pairs={{0,8},{4,12},{16,24},{20,28},{1,9},{5,13},{17,25},{21,29},{2,10},{... | collective-permute-start | bytes 786440 | tf_op jit(solution)/shard_map/ppermute | solution.py:399
  14.7 3.4 %collective-permute-start.3 = (bf16[4,256,128]{2,1,0:T(8,128)(2,1)S(1)}, bf16[4,256,128]{2,1,0:T(8,128)(2,1)S(1)}, u32[]{:S(2)}, u32[]{:S(2)}) collective-permute-start(bf16[4,256,128]{2,1,0:T(8,128)(2,1)S(1)} %fusion.2), channel_id=1, source_target_pairs={{0,16},{4,20},{8,24},{12,28},{1,17},{5,21},{9,25},{13,29},{2,18},{... | collective-permute-start | bytes 786440 | tf_op jit(solution)/shard_map/ppermute | solution.py:399
  18.2 1.3 collective-permute-start.4
  19.5 9.7 %query_side.1 = (bf16[8,1024,256]{2,1,0:T(8,128)(2,1)}, bf16[1024,1024]{1,0:T(8,128)(2,1)}) custom-call(bf16[1024,1024]{1,0:T(8,128)(2,1)} %query_ref.1, bf16[1024,1024]{1,0:T(8,128)(2,1)} %value_ref.3, bf16[8,128,128]{2,1,0:T(8,128)(2,1)S(1)} %copy-done.11, bf16[8,256,1024]{2,1,0:T(8,128)(2,1)} %get-tuple-element.48.key_feat_ref), custom_call_target="tpu_custom_call" | custom-call | tf_op jit(solution)/shard_map/query_side/pallas_call | solution.py:187
  29.8 1.5 %collective-permute-done.5.theirs_ref = bf16[4,256,128]{2,1,0:T(8,128)(2,1)S(1)} collective-permute-done((bf16[4,256,128]{2,1,0:T(8,128)(2,1)S(1)}, bf16[4,256,128]{2,1,0:T(8,128)(2,1)S(1)}, u32[]{:S(2)}, u32[]{:S(2)}) %collective-permute-start.5) | collective-permute-done | bytes 262176 | tf_op jit(solution)/shard_map/ppermute | solution.py:381
  31.3 1.8 %finish.2.x_ref.refs_0_ = bf16[128,1024]{1,0:T(8,128)(2,1)S(1)} custom-call(s32[1]{0:T(128)} %bitcast.1.core_ref, bf16[8,1024,256]{2,1,0:T(8,128)(2,1)} %get-tuple-element.56.feat_ref, bf16[1024,1024]{1,0:T(8,128)(2,1)} %get-tuple-element.51.local_ref, bf16[4,256,128]{2,1,0:T(8,128)(2,1)S(1)} %collective-permute-done.5.theirs_ref, ...), custom_call_target="tpu_custom_call" | custom-call | tf_op jit(solution)/shard_map/finish/pallas_call | solution.py:262
  33.1 2.7 %collective-permute-start.7 = (bf16[128,1024]{1,0:T(8,128)(2,1)S(1)}, bf16[128,1024]{1,0:T(8,128)(2,1)S(1)}, u32[]{:S(2)}, u32[]{:S(2)}) collective-permute-start(bf16[128,1024]{1,0:T(8,128)(2,1)S(1)} %finish.2.x_ref.refs_0_), channel_id=1, source_target_pairs={{0,2},{1,3},{2,0},{3,1},{4,6},{5,7},{6,4},{7,5},{8,10},{9,11},{10,... | collective-permute-start | bytes 786440 | tf_op jit(solution)/shard_map/ppermute | solution.py:381
  35.9 2.5 %collective-permute-start.9 = (bf16[256,1024]{1,0:T(8,128)(2,1)S(1)}, bf16[256,1024]{1,0:T(8,128)(2,1)S(1)}, u32[]{:S(2)}, u32[]{:S(2)}) collective-permute-start(bf16[256,1024]{1,0:T(8,128)(2,1)S(1)} %get-tuple-element.85), channel_id=1, source_target_pairs={{0,16},{4,20},{8,24},{12,28},{16,0},{20,4},{24,8},{28,12},{1,17},{... | collective-permute-start | bytes 1572872 | tf_op jit(solution)/shard_map/ppermute | solution.py:381
  38.5 5.8 %finish.3 = (bf16[128,1024]{1,0:T(8,128)(2,1)}, bf16[128,1024]{1,0:T(8,128)(2,1)}, bf16[128,1024]{1,0:T(8,128)(2,1)}, bf16[128,1024]{1,0:T(8,128)(2,1)}, bf16[12...) custom-call(s32[1]{0:T(128)} %bitcast.1.core_ref, ...), custom_call_target="tpu_custom_call" | custom-call | tf_op jit(solution)/shard_map/finish/pallas_call | solution.py:262
  44.4 3.7 %collective-permute-done.7.y_ref.refs_1_ = bf16[128,1024]{1,0:T(8,128)(2,1)S(1)} collective-permute-done((bf16[128,1024]{1,0:T(8,128)(2,1)S(1)}, bf16[128,1024]{1,0:T(8,128)(2,1)S(1)}, u32[]{:S(2)}, u32[]{:S(2)}) %collective-permute-start.7) | collective-permute-done | bytes 262176 | tf_op jit(solution)/shard_map/ppermute | solution.py:381
  48.1 2.3 %collective-permute-done.9.refs_2_ = bf16[256,1024]{1,0:T(8,128)(2,1)S(1)} collective-permute-done((bf16[256,1024]{1,0:T(8,128)(2,1)S(1)}, bf16[256,1024]{1,0:T(8,128)(2,1)S(1)}, u32[]{:S(2)}, u32[]{:S(2)}) %collective-permute-start.9) | collective-permute-done | bytes 524320 | tf_op jit(solution)/shard_map/ppermute | solution.py:381
  50.4 1.5 collective-permute-done.8.refs_1_
  51.8 1.0 collective-permute-start.6
  52.9 0.9 collective-permute-done.11.refs_4_
  54.5 1.5 %collective-permute-start.13 = (bf16[128,1024]{1,0:T(8,128)(2,1)S(1)}, bf16[128,1024]{1,0:T(8,128)(2,1)S(1)}, u32[]{:S(2)}, u32[]{:S(2)}) collective-permute-start(bf16[128,1024]{1,0:T(8,128)(2,1)S(1)} %partial_product.8), channel_id=1, source_target_pairs={{0,1},{1,0},{2,3},{3,2},{4,5},{5,4},{6,7},{7,6},{8,9},{9,8},{10,11... | collective-permute-start | bytes 786440 | tf_op jit(solution)/shard_map/ppermute | solution.py:381
  56.0 1.2 collective-permute-start.16
  57.1 3.4 %copy-done = bf16[4096,1024]{1,0:T(8,128)(2,1)S(1)} copy-done((bf16[4096,1024]{1,0:T(8,128)(2,1)S(1)}, bf16[4096,1024]{1,0:T(8,128)(2,1)}, u32[]{:S(2)}) %copy-start) | copy-done | bytes 8388632
  60.5 0.7 project.8.a_ref
  61.3 6.5 %collective-permute-done.6.y_ref.refs_1_ = bf16[128,1024]{1,0:T(8,128)(2,1)S(1)} collective-permute-done((bf16[128,1024]{1,0:T(8,128)(2,1)}, bf16[128,1024]{1,0:T(8,128)(2,1)S(1)}, u32[]{:S(2)}, u32[]{:S(2)}) %collective-permute-start.6) | collective-permute-done | bytes 262176 | tf_op jit(solution)/shard_map/ppermute | solution.py:381
  68.6 2.5 %collective-permute-start.14 = (bf16[128,1024]{1,0:T(8,128)(2,1)S(1)}, bf16[128,1024]{1,0:T(8,128)(2,1)S(1)}, u32[]{:S(2)}, u32[]{:S(2)}) collective-permute-start(bf16[128,1024]{1,0:T(8,128)(2,1)S(1)} %copy-done.7), channel_id=1, source_target_pairs={{0,2},{1,3},{2,0},{3,1},{4,6},{5,7},{6,4},{7,5},{8,10},{9,11},{10,... | collective-permute-start | bytes 786440 | tf_op jit(solution)/shard_map/ppermute | solution.py:381
  71.1 7.9 %collective-permute-done.16.y_ref.refs_1_ = bf16[128,1024]{1,0:T(8,128)(2,1)S(1)} collective-permute-done((bf16[128,1024]{1,0:T(8,128)(2,1)S(1)}, bf16[128,1024]{1,0:T(8,128)(2,1)S(1)}, u32[]{:S(2)}, u32[]{:S(2)}) %collective-permute-start.16) | collective-permute-done | bytes 262176 | tf_op jit(solution)/shard_map/ppermute | solution.py:381
  79.9 2.5 %collective-permute-start.20 = (bf16[128,1024]{1,0:T(8,128)(2,1)S(1)}, bf16[128,1024]{1,0:T(8,128)(2,1)S(1)}, u32[]{:S(2)}, u32[]{:S(2)}) collective-permute-start(bf16[128,1024]{1,0:T(8,128)(2,1)S(1)} %partial_product.10), channel_id=1, source_target_pairs={{0,1},{1,0},{2,3},{3,2},{4,5},{5,4},{6,7},{7,6},{8,9},{9,8},{10,11... | collective-permute-start | bytes 786440 | tf_op jit(solution)/shard_map/ppermute | solution.py:381
  83.1 12.8 %collective-permute-done.14.y_ref.refs_1_ = bf16[128,1024]{1,0:T(8,128)(2,1)S(1)} collective-permute-done((bf16[128,1024]{1,0:T(8,128)(2,1)S(1)}, bf16[128,1024]{1,0:T(8,128)(2,1)S(1)}, u32[]{:S(2)}, u32[]{:S(2)}) %collective-permute-start.14) | collective-permute-done | bytes 262176 | tf_op jit(solution)/shard_map/ppermute | solution.py:381
  95.8 0.7 partial_product.11
  96.7 2.1 %collective-permute-start.18 = (bf16[128,1024]{1,0:T(8,128)(2,1)S(1)}, bf16[128,1024]{1,0:T(8,128)(2,1)S(1)}, u32[]{:S(2)}, u32[]{:S(2)}) collective-permute-start(bf16[128,1024]{1,0:T(8,128)(2,1)S(1)} %partial_product.11), channel_id=1, source_target_pairs={{0,1},{1,0},{2,3},{3,2},{4,5},{5,4},{6,7},{7,6},{8,9},{9,8},{10,11... | collective-permute-start | bytes 786440 | tf_op jit(solution)/shard_map/ppermute | solution.py:381
  99.5 7.6 %collective-permute-done.19.y_ref.refs_1_ = bf16[128,1024]{1,0:T(8,128)(2,1)S(1)} collective-permute-done((bf16[128,1024]{1,0:T(8,128)(2,1)S(1)}, bf16[128,1024]{1,0:T(8,128)(2,1)S(1)}, u32[]{:S(2)}, u32[]{:S(2)}) %collective-permute-start.19) | collective-permute-done | bytes 262176 | tf_op jit(solution)/shard_map/ppermute | solution.py:381
  107.2 0.7 partial_product.12
  108.0 2.1 %collective-permute-start.23 = (bf16[128,1024]{1,0:T(8,128)(2,1)S(1)}, bf16[128,1024]{1,0:T(8,128)(2,1)S(1)}, u32[]{:S(2)}, u32[]{:S(2)}) collective-permute-start(bf16[128,1024]{1,0:T(8,128)(2,1)S(1)} %copy-done.4), channel_id=1, source_target_pairs={{0,2},{1,3},{2,0},{3,1},{4,6},{5,7},{6,4},{7,5},{8,10},{9,11},{10,... | collective-permute-start | bytes 786440 | tf_op jit(solution)/shard_map/ppermute | solution.py:381
  110.9 1.9 %collective-permute-done.17.y_ref.refs_1_ = bf16[128,1024]{1,0:T(8,128)(2,1)S(1)} collective-permute-done((bf16[128,1024]{1,0:T(8,128)(2,1)S(1)}, bf16[128,1024]{1,0:T(8,128)(2,1)S(1)}, u32[]{:S(2)}, u32[]{:S(2)}) %collective-permute-start.17) | collective-permute-done | bytes 262176 | tf_op jit(solution)/shard_map/ppermute | solution.py:381
  112.8 2.9 %collective-permute-done.18.b_ref = bf16[128,1024]{1,0:T(8,128)(2,1)S(1)} collective-permute-done((bf16[128,1024]{1,0:T(8,128)(2,1)S(1)}, bf16[128,1024]{1,0:T(8,128)(2,1)S(1)}, u32[]{:S(2)}, u32[]{:S(2)}) %collective-permute-start.18) | collective-permute-done | bytes 262176 | tf_op jit(solution)/shard_map/ppermute | solution.py:381
  115.6 0.7 partial_product.13
  116.5 0.8 join.8.refs_0_
  117.2 0.7 join.9.refs_0_
  118.0 0.8 join.10.refs_0_
  118.9 1.3 collective-permute-start.21
  121.0 5.9 %collective-permute-done.24.b_ref = bf16[128,1024]{1,0:T(8,128)(2,1)S(1)} collective-permute-done((bf16[128,1024]{1,0:T(8,128)(2,1)S(1)}, bf16[128,1024]{1,0:T(8,128)(2,1)S(1)}, u32[]{:S(2)}, u32[]{:S(2)}) %collective-permute-start.24) | collective-permute-done | bytes 262176 | tf_op jit(solution)/shard_map/ppermute | solution.py:381
  128.4 6.6 %collective-permute-done.22.b_ref = bf16[128,1024]{1,0:T(8,128)(2,1)S(1)} collective-permute-done((bf16[128,1024]{1,0:T(8,128)(2,1)S(1)}, bf16[128,1024]{1,0:T(8,128)(2,1)S(1)}, u32[]{:S(2)}, u32[]{:S(2)}) %collective-permute-start.22) | collective-permute-done | bytes 262176 | tf_op jit(solution)/shard_map/ppermute | solution.py:381
  135.8 0.8 project.15.a_ref
  136.6 0.8 join.11.refs_0_
  137.3 0.7 join.12.refs_0_
  138.1 0.7 project.12.a_ref
  138.8 0.8 join.13.refs_0_
  139.6 1.0 collective-permute-done.26.b_ref
  140.6 0.7 join.14.refs_0_
  141.3 4.9 %collective-permute-done.25.b_ref = bf16[128,1024]{1,0:T(8,128)(2,1)S(1)} collective-permute-done((bf16[128,1024]{1,0:T(8,128)(2,1)S(1)}, bf16[128,1024]{1,0:T(8,128)(2,1)S(1)}, u32[]{:S(2)}, u32[]{:S(2)}) %collective-permute-start.25) | collective-permute-done | bytes 262176 | tf_op jit(solution)/shard_map/ppermute | solution.py:381
  146.2 0.8 join.15
  (63 shorter events, 9.3 us)
Async XLA Ops:
  0.0 19.5 %copy-start.11 = (bf16[8,128,128]{2,1,0:T(8,128)(2,1)S(1)}, bf16[8,128,128]{2,1,0:T(8,128)(2,1)}, u32[]{:S(2)}) copy-start(bf16[8,128,128]{2,1,0:T(8,128)(2,1)} %freq_ref.2) | copy-start | bytes 786436
  8.1 3.1 %collective-permute-start = (bf16[4,256,128]{2,1,0:T(8,128)(2,1)S(1)}, bf16[4,256,128]{2,1,0:T(8,128)(2,1)S(1)}, u32[]{:S(2)}, u32[]{:S(2)}) collective-permute-start(bf16[4,256,128]{2,1,0:T(8,128)(2,1)S(1)} %get-tuple-element.46), channel_id=1, source_target_pairs={{0,4},{4,0},{8,12},{12,8},{16,20},{20,16},{24,28},{28,24},{1,5},{5... | collective-permute-start | bytes 786440 | tf_op jit(solution)/shard_map/ppermute | solution.py:381
  8.6 27.1 %collective-permute-start.1 = (bf16[512,1024]{1,0:T(8,128)(2,1)}, bf16[512,1024]{1,0:T(8,128)(2,1)S(1)}, u32[]{:S(2)}, u32[]{:S(2)}) collective-permute-start(bf16[512,1024]{1,0:T(8,128)(2,1)} %get-tuple-element.50), channel_id=1, source_target_pairs={{0,1},{1,0},{2,3},{3,2},{4,5},{5,4},{6,7},{7,6},{8,9},{9,8},{10,11... | collective-permute-start | bytes 3145736 | tf_op jit(solution)/shard_map/ppermute | solution.py:381
  11.3 18.0 %collective-permute-start.2 = (bf16[4,256,128]{2,1,0:T(8,128)(2,1)S(1)}, bf16[4,256,128]{2,1,0:T(8,128)(2,1)S(1)}, u32[]{:S(2)}, u32[]{:S(2)}) collective-permute-start(bf16[4,256,128]{2,1,0:T(8,128)(2,1)S(1)} %fusion.2), channel_id=1, source_target_pairs={{0,8},{4,12},{16,24},{20,28},{1,9},{5,13},{17,25},{21,29},{2,10},{... | collective-permute-start | bytes 786440 | tf_op jit(solution)/shard_map/ppermute | solution.py:399
  14.7 14.6 %collective-permute-start.3 = (bf16[4,256,128]{2,1,0:T(8,128)(2,1)S(1)}, bf16[4,256,128]{2,1,0:T(8,128)(2,1)S(1)}, u32[]{:S(2)}, u32[]{:S(2)}) collective-permute-start(bf16[4,256,128]{2,1,0:T(8,128)(2,1)S(1)} %fusion.2), channel_id=1, source_target_pairs={{0,16},{4,20},{8,24},{12,28},{1,17},{5,21},{9,25},{13,29},{2,18},{... | collective-permute-start | bytes 786440 | tf_op jit(solution)/shard_map/ppermute | solution.py:399
  18.2 11.2 %collective-permute-start.4 = (bf16[4,256,128]{2,1,0:T(8,128)(2,1)S(1)}, bf16[4,256,128]{2,1,0:T(8,128)(2,1)S(1)}, u32[]{:S(2)}, u32[]{:S(2)}) collective-permute-start(bf16[4,256,128]{2,1,0:T(8,128)(2,1)S(1)} %fusion.2), channel_id=1, source_target_pairs={{0,24},{4,28},{8,16},{12,20},{1,25},{5,29},{9,17},{13,21},{2,26},{... | collective-permute-start | bytes 786440 | tf_op jit(solution)/shard_map/ppermute | solution.py:399
  19.5 11.8 %copy-start.12 = (bf16[1024]{0:T(1024)(128)(2,1)S(1)}, bf16[1024]{0:T(1024)(128)(2,1)}, u32[]{:S(2)}) copy-start(bf16[1024]{0:T(1024)(128)(2,1)} %param.10) | copy-start | bytes 6148
  29.7 3.4 %copy-start.2 = (bf16[4,256,128]{2,1,0:T(8,128)(2,1)}, bf16[4,256,128]{2,1,0:T(8,128)(2,1)S(1)}, u32[]{:S(2)}) copy-start(bf16[4,256,128]{2,1,0:T(8,128)(2,1)S(1)} %get-tuple-element.87.mine_ref) | copy-start | bytes 786436
  29.7 1.6 %collective-permute-start.5 = (bf16[4,256,128]{2,1,0:T(8,128)(2,1)S(1)}, bf16[4,256,128]{2,1,0:T(8,128)(2,1)S(1)}, u32[]{:S(2)}, u32[]{:S(2)}) collective-permute-start(bf16[4,256,128]{2,1,0:T(8,128)(2,1)S(1)} %get-tuple-element.88), channel_id=1, source_target_pairs={{0,4},{4,0},{8,12},{12,8},{16,20},{20,16},{24,28},{28,24},{1,5},{5... | collective-permute-start | bytes 786440 | tf_op jit(solution)/shard_map/ppermute | solution.py:381
  31.3 1.8 %copy-start.10 = (bf16[4,256,128]{2,1,0:T(8,128)(2,1)}, bf16[4,256,128]{2,1,0:T(8,128)(2,1)S(1)}, u32[]{:S(2)}) copy-start(bf16[4,256,128]{2,1,0:T(8,128)(2,1)S(1)} %collective-permute-done.5.theirs_ref) | copy-start | bytes 786436
  33.1 14.9 %collective-permute-start.7 = (bf16[128,1024]{1,0:T(8,128)(2,1)S(1)}, bf16[128,1024]{1,0:T(8,128)(2,1)S(1)}, u32[]{:S(2)}, u32[]{:S(2)}) collective-permute-start(bf16[128,1024]{1,0:T(8,128)(2,1)S(1)} %finish.2.x_ref.refs_0_), channel_id=1, source_target_pairs={{0,2},{1,3},{2,0},{3,1},{4,6},{5,7},{6,4},{7,5},{8,10},{9,11},{10,... | collective-permute-start | bytes 786440 | tf_op jit(solution)/shard_map/ppermute | solution.py:381
  35.9 14.5 %collective-permute-start.9 = (bf16[256,1024]{1,0:T(8,128)(2,1)S(1)}, bf16[256,1024]{1,0:T(8,128)(2,1)S(1)}, u32[]{:S(2)}, u32[]{:S(2)}) collective-permute-start(bf16[256,1024]{1,0:T(8,128)(2,1)S(1)} %get-tuple-element.85), channel_id=1, source_target_pairs={{0,16},{4,20},{8,24},{12,28},{16,0},{20,4},{24,8},{28,12},{1,17},{... | collective-permute-start | bytes 1572872 | tf_op jit(solution)/shard_map/ppermute | solution.py:381
  38.4 13.4 %collective-permute-start.8 = (bf16[256,1024]{1,0:T(8,128)(2,1)S(1)}, bf16[256,1024]{1,0:T(8,128)(2,1)S(1)}, u32[]{:S(2)}, u32[]{:S(2)}) collective-permute-start(bf16[256,1024]{1,0:T(8,128)(2,1)S(1)} %get-tuple-element.86), channel_id=1, source_target_pairs={{0,8},{4,12},{8,0},{12,4},{16,24},{20,28},{24,16},{28,20},{1,9},{5... | collective-permute-start | bytes 1572872 | tf_op jit(solution)/shard_map/ppermute | solution.py:381
  48.1 5.7 %collective-permute-start.10 = (bf16[512,1024]{1,0:T(8,128)(2,1)S(1)}, bf16[512,1024]{1,0:T(8,128)(2,1)S(1)}, u32[]{:S(2)}, u32[]{:S(2)}) collective-permute-start(bf16[512,1024]{1,0:T(8,128)(2,1)S(1)} %collective-permute-done.1.refs_0_), channel_id=1, source_target_pairs={{0,4},{4,0},{8,12},{12,8},{16,20},{20,16},{24,28},{28,24},{1,5},{5... | collective-permute-start | bytes 3145736 | tf_op jit(solution)/shard_map/ppermute | solution.py:381
  50.4 2.5 %collective-permute-start.12 = (bf16[256,1024]{1,0:T(8,128)(2,1)S(1)}, bf16[256,1024]{1,0:T(8,128)(2,1)S(1)}, u32[]{:S(2)}, u32[]{:S(2)}) collective-permute-start(bf16[256,1024]{1,0:T(8,128)(2,1)S(1)} %collective-permute-done.9.refs_2_), channel_id=1, source_target_pairs={{0,4},{4,0},{8,12},{12,8},{16,20},{20,16},{24,28},{28,24},{1,5},{5... | collective-permute-start | bytes 1572872 | tf_op jit(solution)/shard_map/ppermute | solution.py:381
  51.8 1.9 %collective-permute-start.11 = (bf16[256,1024]{1,0:T(8,128)(2,1)S(1)}, bf16[256,1024]{1,0:T(8,128)(2,1)S(1)}, u32[]{:S(2)}, u32[]{:S(2)}) collective-permute-start(bf16[256,1024]{1,0:T(8,128)(2,1)S(1)} %collective-permute-done.8.refs_1_), channel_id=1, source_target_pairs={{0,4},{4,0},{8,12},{12,8},{16,20},{20,16},{24,28},{28,24},{1,5},{5... | collective-permute-start | bytes 1572872 | tf_op jit(solution)/shard_map/ppermute | solution.py:381
  51.8 4.2 %copy-start.8 = (bf16[128,1024]{1,0:T(8,128)(2,1)S(1)}, bf16[128,1024]{1,0:T(8,128)(2,1)}, u32[]{:S(2)}) copy-start(bf16[128,1024]{1,0:T(8,128)(2,1)} %get-tuple-element.67.x_ref.refs_0_) | copy-start | bytes 786436
  51.8 15.9 %collective-permute-start.6 = (bf16[128,1024]{1,0:T(8,128)(2,1)}, bf16[128,1024]{1,0:T(8,128)(2,1)S(1)}, u32[]{:S(2)}, u32[]{:S(2)}) collective-permute-start(bf16[128,1024]{1,0:T(8,128)(2,1)} %get-tuple-element.61.x_ref.refs_0_), channel_id=1, source_target_pairs={{0,2},{1,3},{2,0},{3,1},{4,6},{5,7},{6,4},{7,5},{8,10},{9,11},{10,... | collective-permute-start | bytes 786440 | tf_op jit(solution)/shard_map/ppermute | solution.py:381
  54.5 14.1 %collective-permute-start.13 = (bf16[128,1024]{1,0:T(8,128)(2,1)S(1)}, bf16[128,1024]{1,0:T(8,128)(2,1)S(1)}, u32[]{:S(2)}, u32[]{:S(2)}) collective-permute-start(bf16[128,1024]{1,0:T(8,128)(2,1)S(1)} %partial_product.8), channel_id=1, source_target_pairs={{0,1},{1,0},{2,3},{3,2},{4,5},{5,4},{6,7},{7,6},{8,9},{9,8},{10,11... | collective-permute-start | bytes 786440 | tf_op jit(solution)/shard_map/ppermute | solution.py:381
  56.0 23.1 %collective-permute-start.16 = (bf16[128,1024]{1,0:T(8,128)(2,1)S(1)}, bf16[128,1024]{1,0:T(8,128)(2,1)S(1)}, u32[]{:S(2)}, u32[]{:S(2)}) collective-permute-start(bf16[128,1024]{1,0:T(8,128)(2,1)S(1)} %copy-done.8), channel_id=1, source_target_pairs={{0,2},{1,3},{2,0},{3,1},{4,6},{5,7},{6,4},{7,5},{8,10},{9,11},{10,... | collective-permute-start | bytes 786440 | tf_op jit(solution)/shard_map/ppermute | solution.py:381
  57.1 3.4 %copy-start = (bf16[4096,1024]{1,0:T(8,128)(2,1)S(1)}, bf16[4096,1024]{1,0:T(8,128)(2,1)}, u32[]{:S(2)}) copy-start(bf16[4096,1024]{1,0:T(8,128)(2,1)} %refs_3_.15) | copy-start | bytes 25165828
  60.5 7.2 %copy-start.9 = (bf16[128,1024]{1,0:T(8,128)(2,1)S(1)}, bf16[128,1024]{1,0:T(8,128)(2,1)}, u32[]{:S(2)}) copy-start(bf16[128,1024]{1,0:T(8,128)(2,1)} %get-tuple-element.61.x_ref.refs_0_) | copy-start | bytes 786436
  61.3 7.3 %copy-start.7 = (bf16[128,1024]{1,0:T(8,128)(2,1)S(1)}, bf16[128,1024]{1,0:T(8,128)(2,1)}, u32[]{:S(2)}) copy-start(bf16[128,1024]{1,0:T(8,128)(2,1)} %get-tuple-element.66.x_ref.refs_0_) | copy-start | bytes 786436
  67.8 14.6 %copy-start.1 = (bf16[4096,1024]{1,0:T(8,128)(2,1)S(1)}, bf16[4096,1024]{1,0:T(8,128)(2,1)}, u32[]{:S(2)}) copy-start(bf16[4096,1024]{1,0:T(8,128)(2,1)} %refs_3_.15) | copy-start | bytes 25165828
  68.5 14.6 %collective-permute-start.15 = (bf16[128,1024]{1,0:T(8,128)(2,1)S(1)}, bf16[128,1024]{1,0:T(8,128)(2,1)S(1)}, u32[]{:S(2)}, u32[]{:S(2)}) collective-permute-start(bf16[128,1024]{1,0:T(8,128)(2,1)S(1)} %partial_product.9), channel_id=1, source_target_pairs={{0,1},{1,0},{2,3},{3,2},{4,5},{5,4},{6,7},{7,6},{8,9},{9,8},{10,11... | collective-permute-start | bytes 786440 | tf_op jit(solution)/shard_map/ppermute | solution.py:381
  68.6 11.2 %copy-start.6 = (bf16[128,1024]{1,0:T(8,128)(2,1)S(1)}, bf16[128,1024]{1,0:T(8,128)(2,1)}, u32[]{:S(2)}) copy-start(bf16[128,1024]{1,0:T(8,128)(2,1)} %get-tuple-element.72.x_ref.refs_0_) | copy-start | bytes 786436
  68.6 27.2 %collective-permute-start.14 = (bf16[128,1024]{1,0:T(8,128)(2,1)S(1)}, bf16[128,1024]{1,0:T(8,128)(2,1)S(1)}, u32[]{:S(2)}, u32[]{:S(2)}) collective-permute-start(bf16[128,1024]{1,0:T(8,128)(2,1)S(1)} %copy-done.7), channel_id=1, source_target_pairs={{0,2},{1,3},{2,0},{3,1},{4,6},{5,7},{6,4},{7,5},{8,10},{9,11},{10,... | collective-permute-start | bytes 786440 | tf_op jit(solution)/shard_map/ppermute | solution.py:381
  79.8 27.4 %collective-permute-start.19 = (bf16[128,1024]{1,0:T(8,128)(2,1)S(1)}, bf16[128,1024]{1,0:T(8,128)(2,1)S(1)}, u32[]{:S(2)}, u32[]{:S(2)}) collective-permute-start(bf16[128,1024]{1,0:T(8,128)(2,1)S(1)} %copy-done.6), channel_id=1, source_target_pairs={{0,2},{1,3},{2,0},{3,1},{4,6},{5,7},{6,4},{7,5},{8,10},{9,11},{10,... | collective-permute-start | bytes 786440 | tf_op jit(solution)/shard_map/ppermute | solution.py:381
  79.9 27.3 %collective-permute-start.20 = (bf16[128,1024]{1,0:T(8,128)(2,1)S(1)}, bf16[128,1024]{1,0:T(8,128)(2,1)S(1)}, u32[]{:S(2)}, u32[]{:S(2)}) collective-permute-start(bf16[128,1024]{1,0:T(8,128)(2,1)S(1)} %partial_product.10), channel_id=1, source_target_pairs={{0,1},{1,0},{2,3},{3,2},{4,5},{5,4},{6,7},{7,6},{8,9},{9,8},{10,11... | collective-permute-start | bytes 786440 | tf_op jit(solution)/shard_map/ppermute | solution.py:381
  83.1 13.5 %copy-start.5 = (bf16[128,1024]{1,0:T(8,128)(2,1)S(1)}, bf16[128,1024]{1,0:T(8,128)(2,1)}, u32[]{:S(2)}) copy-start(bf16[128,1024]{1,0:T(8,128)(2,1)} %get-tuple-element.70.x_ref.refs_0_) | copy-start | bytes 786436
  96.6 16.2 %collective-permute-start.17 = (bf16[128,1024]{1,0:T(8,128)(2,1)S(1)}, bf16[128,1024]{1,0:T(8,128)(2,1)S(1)}, u32[]{:S(2)}, u32[]{:S(2)}) collective-permute-start(bf16[128,1024]{1,0:T(8,128)(2,1)S(1)} %copy-done.5), channel_id=1, source_target_pairs={{0,2},{1,3},{2,0},{3,1},{4,6},{5,7},{6,4},{7,5},{8,10},{9,11},{10,... | collective-permute-start | bytes 786440 | tf_op jit(solution)/shard_map/ppermute | solution.py:381
  96.7 19.0 %collective-permute-start.18 = (bf16[128,1024]{1,0:T(8,128)(2,1)S(1)}, bf16[128,1024]{1,0:T(8,128)(2,1)S(1)}, u32[]{:S(2)}, u32[]{:S(2)}) collective-permute-start(bf16[128,1024]{1,0:T(8,128)(2,1)S(1)} %partial_product.11), channel_id=1, source_target_pairs={{0,1},{1,0},{2,3},{3,2},{4,5},{5,4},{6,7},{7,6},{8,9},{9,8},{10,11... | collective-permute-start | bytes 786440 | tf_op jit(solution)/shard_map/ppermute | solution.py:381
  99.5 8.5 %copy-start.4 = (bf16[128,1024]{1,0:T(8,128)(2,1)S(1)}, bf16[128,1024]{1,0:T(8,128)(2,1)}, u32[]{:S(2)}) copy-start(bf16[128,1024]{1,0:T(8,128)(2,1)} %get-tuple-element.81.x_ref.refs_0_) | copy-start | bytes 786436
  107.9 18.9 %collective-permute-start.24 = (bf16[128,1024]{1,0:T(8,128)(2,1)S(1)}, bf16[128,1024]{1,0:T(8,128)(2,1)S(1)}, u32[]{:S(2)}, u32[]{:S(2)}) collective-permute-start(bf16[128,1024]{1,0:T(8,128)(2,1)S(1)} %partial_product.12), channel_id=1, source_target_pairs={{0,1},{1,0},{2,3},{3,2},{4,5},{5,4},{6,7},{7,6},{8,9},{9,8},{10,11... | collective-permute-start | bytes 786440 | tf_op jit(solution)/shard_map/ppermute | solution.py:381
  108.0 18.8 %collective-permute-start.23 = (bf16[128,1024]{1,0:T(8,128)(2,1)S(1)}, bf16[128,1024]{1,0:T(8,128)(2,1)S(1)}, u32[]{:S(2)}, u32[]{:S(2)}) collective-permute-start(bf16[128,1024]{1,0:T(8,128)(2,1)S(1)} %copy-done.4), channel_id=1, source_target_pairs={{0,2},{1,3},{2,0},{3,1},{4,6},{5,7},{6,4},{7,5},{8,10},{9,11},{10,... | collective-permute-start | bytes 786440 | tf_op jit(solution)/shard_map/ppermute | solution.py:381
  116.4 18.6 %collective-permute-start.22 = (bf16[128,1024]{1,0:T(8,128)(2,1)S(1)}, bf16[128,1024]{1,0:T(8,128)(2,1)S(1)}, u32[]{:S(2)}, u32[]{:S(2)}) collective-permute-start(bf16[128,1024]{1,0:T(8,128)(2,1)S(1)} %partial_product.13), channel_id=1, source_target_pairs={{0,1},{1,0},{2,3},{3,2},{4,5},{5,4},{6,7},{7,6},{8,9},{9,8},{10,11... | collective-permute-start | bytes 786440 | tf_op jit(solution)/shard_map/ppermute | solution.py:381
  118.0 0.9 copy-start.3
  118.9 16.0 %collective-permute-start.21 = (bf16[128,1024]{1,0:T(8,128)(2,1)S(1)}, bf16[128,1024]{1,0:T(8,128)(2,1)S(1)}, u32[]{:S(2)}, u32[]{:S(2)}) collective-permute-start(bf16[128,1024]{1,0:T(8,128)(2,1)S(1)} %copy-done.3), channel_id=1, source_target_pairs={{0,2},{1,3},{2,0},{3,1},{4,6},{5,7},{6,4},{7,5},{8,10},{9,11},{10,... | collective-permute-start | bytes 786440 | tf_op jit(solution)/shard_map/ppermute | solution.py:381
  127.6 13.0 %collective-permute-start.26 = (bf16[128,1024]{1,0:T(8,128)(2,1)S(1)}, bf16[128,1024]{1,0:T(8,128)(2,1)S(1)}, u32[]{:S(2)}, u32[]{:S(2)}) collective-permute-start(bf16[128,1024]{1,0:T(8,128)(2,1)S(1)} %partial_product.14), channel_id=1, source_target_pairs={{0,1},{1,0},{2,3},{3,2},{4,5},{5,4},{6,7},{7,6},{8,9},{9,8},{10,11... | collective-permute-start | bytes 786440 | tf_op jit(solution)/shard_map/ppermute | solution.py:381
  135.7 10.5 %collective-permute-start.25 = (bf16[128,1024]{1,0:T(8,128)(2,1)S(1)}, bf16[128,1024]{1,0:T(8,128)(2,1)S(1)}, u32[]{:S(2)}, u32[]{:S(2)}) collective-permute-start(bf16[128,1024]{1,0:T(8,128)(2,1)S(1)} %partial_product.15), channel_id=1, source_target_pairs={{0,1},{1,0},{2,3},{3,2},{4,5},{5,4},{6,7},{7,6},{8,9},{9,8},{10,11... | collective-permute-start | bytes 786440 | tf_op jit(solution)/shard_map/ppermute | solution.py:381
